TPU v7x, 32 devices: a whole 2x2x4 slice. The times are simulated.
32 devices in a mesh: blk: 8 (over z, x), col: 4 (over y, core).
Axes of the slice: x: 2, y: 2, z: 4, core: 2. Of those that a mesh axis runs over, the one named last changes fastest.
Arguments:
- slab: float32 [16384, 1024], P('blk', 'col'), may hold values from -6 to 6
- angles: float32 [4, 8192], P(None, 'blk'), may hold values from -3.140625 to 3.140625
- pairing: int32 [4], replicated, may hold values from 0 to 1, as said below
- band_offsets: int32 [8], replicated, may hold values from 1 to 512, as said below
- band_weights: float32 [8], replicated, may hold values from -0.0625 to 0.0625
Outputs:
- evolved: float32 [16384, 1024], P('blk', 'col')
- angle_gradient: float32 [4, 8192], P(None, 'blk')
Inputs may be any that keep to these rules, and one draw needn't show every extreme that they name: `pairing`: the entries alternate between 0 and 1 from one layer to the next. `band_offsets`: exactly one entry equals 512.
All inputs are finite; a program needn't handle non-finite values.
Results may differ from a plain program's by a relative error of at most 0.0001.
Values sent between devices are 32-bit elements; how exact they have to be, the bound alone decides.
A program may use at most 128 MiB of HBM per device.

v0:
```python
import jax
import jax.numpy as jnp
from jax import lax
from jax.sharding import PartitionSpec as P

SITES_DEV = 1024
LAYERS = 4
REACH = 512
BANDS = 8


def with_halo(cells, sides, width):
    for axis, dim in sides:
        count = lax.axis_size(axis)
        head = lax.slice_in_dim(cells, 0, width, axis=dim)
        tail = lax.slice_in_dim(cells, cells.shape[dim] - width, cells.shape[dim], axis=dim)
        cells = jnp.concatenate(
            [
                lax.ppermute(tail, axis, [(i, (i + 1) % count) for i in range(count)]),
                cells,
                lax.ppermute(head, axis, [((i + 1) % count, i) for i in range(count)]),
            ],
            axis=dim,
        )
    return cells


def shifted(value, axis, steps):
    count = lax.axis_size(axis)
    pairs = [(source, (source + steps) % count) for source in range(count)]
    return lax.ppermute(value, axis, pairs)


def rotate_frame(stack, cosine, sine, offset):
    fields, rows, width = stack.shape
    padded = jnp.concatenate([stack, jnp.zeros((fields, 1, width), stack.dtype)], 1)
    window = lax.dynamic_slice_in_dim(padded, offset, rows, 1).reshape(fields, rows // 2, 2, width)
    first = window[:, :, 0]
    second = window[:, :, 1]
    cos_b = cosine[None, :, None]
    sin_b = sine[None, :, None]
    new_first = cos_b * first - sin_b * second
    new_second = sin_b * first + cos_b * second
    flat = jnp.stack([new_first, new_second], 2).reshape(fields, rows, width)
    joined = jnp.concatenate([stack[:, :1], flat], 1)
    return (lax.dynamic_slice_in_dim(joined, 1 - offset, rows, 1), first, second)


def pair_gradient(first, second, margin):
    whole = jnp.sum(second[0] * first[1] - first[0] * second[1], axis=1)
    return whole[margin // 2 : margin // 2 + SITES_DEV]


def wide_rims(stack, width):
    return with_halo(stack, (("blk", 1),), width)


def layer_step(stack, cosine, sine, offset):
    fields, rows, width = stack.shape
    following = shifted(stack[:, :1], "blk", -1)
    blank = jnp.zeros((fields, 1, width), stack.dtype)
    frame = jnp.concatenate([blank, blank, stack, following, blank], 1)
    turned, first, second = rotate_frame(frame, cosine, sine, offset)
    returned = shifted(turned[:, rows + 2 : rows + 3], "blk", 1)
    leading = jnp.where(offset == 1, returned, turned[:, 2:3])
    fresh = jnp.concatenate([leading, turned[:, 3 : 2 + rows]], 1)
    return (fresh, first, second)


def band_adjoint(rows_ext, start, count, band_offsets, band_weights):
    total = jnp.zeros((count, rows_ext.shape[1]), jnp.float32)
    for band in range(BANDS):
        reach = band_offsets[band]
        upper = lax.dynamic_slice_in_dim(rows_ext, start + reach, count, 0)
        lower = lax.dynamic_slice_in_dim(rows_ext, start - reach, count, 0)
        total = total + band_weights[band] * (upper + lower)
    return total


def on_device(slab, angles, pairing, band_offsets, band_weights):
    rows = slab.shape[0]
    padding = jnp.zeros_like(angles[:, :1])
    angle_ext = jnp.concatenate([padding, angles, padding], 1)
    cosines = jnp.cos(angle_ext)
    sines = jnp.sin(angle_ext)
    locals_grad = [None] * LAYERS
    stack = slab[None]
    for layer in range(LAYERS):
        stack, first, second = layer_step(stack, cosines[layer], sines[layer], pairing[layer])
    evolved = stack[0]
    band = wide_rims(stack, REACH)[0]
    adjoint = band_adjoint(band, REACH, rows, band_offsets, band_weights)
    fields = jnp.stack([adjoint, evolved])
    for layer in reversed(range(LAYERS)):
        fields, first, second = layer_step(fields, cosines[layer], -sines[layer], pairing[layer])
        locals_grad[layer] = pair_gradient(first, second, 2)
    summed = [lax.psum(part_grad, "col") for part_grad in locals_grad]
    gradient = jnp.stack(summed)
    return (evolved, gradient)


def solution(mesh):
    in_specs = (P("blk", "col"), P(None, "blk"), P(), P(), P())
    out_specs = (P("blk", "col"), P(None, "blk"))
    return jax.shard_map(
        on_device, mesh=mesh, in_specs=in_specs, out_specs=out_specs, check_vma=False
    )
```

profile of v0, /device:TPU:0, one launch (start us, length us, event | category | flops | bytes accessed | tf_op | source)
XLA Modules:
  0.0 296.0 jit_solution(8310431892935492917)
XLA Ops:
  1.3 6.0 %collective-permute-start = (f32[1,1,256]{2,1,0:T(1,128)S(1)}, f32[1,1,256]{2,1,0:T(1,128)S(1)}, u32[]{:S(2)}, u32[]{:S(2)}) collective-permute-start(f32[1,1,256]{2,1,0:T(1,128)S(1)} %slice.421), channel_id=1, source_target_pairs={{0,28},{4,0},{8,4},{12,8},{16,12},{20,16},{24,20},{28,24},{1,29},{... | collective-permute-start | bytes 3080 | tf_op jit(solution)/shard_map/ppermute | solution.py:31
  49.8 8.2 %concatenate.56 = f32[1,2053,256]{2,1,0:T(8,128)} concatenate(f32[1,2,256]{2,1,0:T(2,128)S(1)} %broadcast.118.clone, f32[1,2048,256]{2,1,0:T(8,128)} %bitcast.101, f32[1,1,256]{2,1,0:T(1,128)S(1)} %collective-permute-done, f32[1,2,256]{2,1,0:T(2,128)S(1)} %broadcast.118.clone), dimensions={1} | concatenate | bytes 4204544 | tf_op jit(solution)/shard_map/concatenate | solution.py:36
  59.7 3.5 %reshape.335 = f32[1,1026,2,256]{3,0,2,1:T(1,128)} reshape(f32[1,2052,256]{2,1,0:T(8,128)S(1)} %constant_dynamic-slice_fusion.7) | data formatting | bytes 4202496 | tf_op jit(solution)/shard_map/reshape | solution.py:37
  63.2 6.6 %multiply_subtract_fusion.6 = (f32[1,1026,1,256]{3,0,2,1:T(1,128)S(1)}, f32[1,1026,1,256]{3,0,2,1:T(1,128)S(1)}) fusion(f32[1,1026,2,256]{3,0,2,1:T(1,128)} %reshape.335, f32[1026]{0:T(1024)S(1)} %get-tuple-element.9, f32[1026]{0:T(1024)S(1)} %get-tuple-element.64), kind=kLoop, calls=%fused_computation.55 | loop fusion | flops 1575936 | bytes 4210704 | tf_op jit(solution)/shard_map/sub | solution.py:42
  72.6 5.5 %collective-permute-done.1 = f32[1,1,256]{2,0,1:T(1,128)S(1)} collective-permute-done((f32[1,1,256]{2,0,1:T(1,128)S(1)}, f32[1,1,256]{2,0,1:T(1,128)S(1)}, u32[]{:S(2)}, u32[]{:S(2)}) %collective-permute-start.1) | collective-permute-done | bytes 1056 | tf_op jit(solution)/shard_map/ppermute | solution.py:31
  83.3 3.2 %constant_dynamic-slice_fusion.6 = f32[1,2052,256]{2,0,1:T(1,128)S(1)} fusion(f32[1,2053,256]{2,0,1:T(1,128)} %constant_dynamic-update-slice_fusion, s32[]{:T(128)S(6)} %select_n.132), kind=kLoop, calls=%fused_computation.98 | loop fusion | bytes 4202500 | tf_op jit(solution)/shard_map/dynamic_slice | solution.py:37
  86.6 4.0 %multiply_subtract_fusion.5 = (f32[1,1026,1,256]{3,0,2,1:T(1,128)S(1)}, f32[1,1026,1,256]{3,0,2,1:T(1,128)S(1)}) fusion(f32[1,1026,2,256]{3,0,2,1:T(1,128)S(1)} %bitcast.92, f32[1026]{0:T(1024)S(1)} %get-tuple-element.8, f32[1026]{0:T(1024)S(1)} %get-tuple-element.63), kind=kLoop, calls=%fused_computation.53 | loop fusion | flops 1575936 | bytes 4210704 | tf_op jit(solution)/shard_map/sub | solution.py:42
  95.0 3.8 %collective-permute-done.3 = f32[1,1,256]{2,0,1:T(1,128)S(1)} collective-permute-done((f32[1,1,256]{2,0,1:T(1,128)S(1)}, f32[1,1,256]{2,0,1:T(1,128)S(1)}, u32[]{:S(2)}, u32[]{:S(2)}) %collective-permute-start.3) | collective-permute-done | bytes 1056 | tf_op jit(solution)/shard_map/ppermute | solution.py:31
  104.2 3.2 %constant_dynamic-slice_fusion.5 = f32[1,2052,256]{2,0,1:T(1,128)S(1)} fusion(f32[1,2053,256]{2,0,1:T(1,128)} %constant_dynamic-update-slice_fusion.4, s32[]{:T(128)S(6)} %select_n.135), kind=kLoop, calls=%fused_computation.97 | loop fusion | bytes 4202500 | tf_op jit(solution)/shard_map/dynamic_slice | solution.py:37
  107.4 4.0 %multiply_subtract_fusion.4 = (f32[1,1026,1,256]{3,0,2,1:T(1,128)S(1)}, f32[1,1026,1,256]{3,0,2,1:T(1,128)S(1)}) fusion(f32[1,1026,2,256]{3,0,2,1:T(1,128)S(1)} %bitcast.93, f32[1026]{0:T(1024)S(1)} %get-tuple-element.7, f32[1026]{0:T(1024)S(1)} %get-tuple-element.62), kind=kLoop, calls=%fused_computation.51 | loop fusion | flops 1575936 | bytes 4210704 | tf_op jit(solution)/shard_map/sub | solution.py:42
  114.6 5.0 %collective-permute-done.5 = f32[1,1,256]{2,0,1:T(1,128)S(1)} collective-permute-done((f32[1,1,256]{2,0,1:T(1,128)S(1)}, f32[1,1,256]{2,0,1:T(1,128)S(1)}, u32[]{:S(2)}, u32[]{:S(2)}) %collective-permute-start.5) | collective-permute-done | bytes 1056 | tf_op jit(solution)/shard_map/ppermute | solution.py:31
  124.9 3.2 %constant_dynamic-slice_fusion.4 = f32[1,2052,256]{2,0,1:T(1,128)S(1)} fusion(f32[1,2053,256]{2,0,1:T(1,128)} %constant_dynamic-update-slice_fusion.8, s32[]{:T(128)S(6)} %select_n.138), kind=kLoop, calls=%fused_computation.96 | loop fusion | bytes 4202500 | tf_op jit(solution)/shard_map/dynamic_slice | solution.py:37
  128.2 4.0 %multiply_subtract_fusion.3 = (f32[1,1026,1,256]{3,0,2,1:T(1,128)S(1)}, f32[1,1026,1,256]{3,0,2,1:T(1,128)S(1)}) fusion(f32[1,1026,2,256]{3,0,2,1:T(1,128)S(1)} %bitcast.91, f32[1026]{0:T(1024)S(1)} %get-tuple-element.6, f32[1026]{0:T(1024)S(1)} %get-tuple-element.65), kind=kLoop, calls=%fused_computation.49 | loop fusion | flops 1575936 | bytes 4210704 | tf_op jit(solution)/shard_map/sub | solution.py:42
  136.1 5.0 %collective-permute-done.7 = f32[1,1,256]{2,1,0:T(1,128)S(1)} collective-permute-done((f32[1,1,256]{2,1,0:T(1,128)S(1)}, f32[1,1,256]{2,1,0:T(1,128)S(1)}, u32[]{:S(2)}, u32[]{:S(2)}) %collective-permute-start.7) | collective-permute-done | bytes 1056 | tf_op jit(solution)/shard_map/ppermute | solution.py:31
  141.2 5.3 %collective-permute-start.9 = (f32[1,512,256]{2,1,0:T(8,128)S(1)}, f32[1,512,256]{2,1,0:T(8,128)}, u32[]{:S(2)}, u32[]{:S(2)}) collective-permute-start(f32[1,512,256]{2,1,0:T(8,128)S(1)} %fusion.8), channel_id=1, source_target_pairs={{4,0},{8,4},{12,8},{16,12},{20,16},{24,20},{28,24},{0,28},{5,1},{9... | collective-permute-start | bytes 1572872 | tf_op jit(solution)/shard_map/ppermute | solution.py:21
  149.4 3.8 %collective-permute-done.8 = f32[1,512,256]{2,1,0:T(8,128)S(1)} collective-permute-done((f32[1,512,256]{2,1,0:T(8,128)S(1)}, f32[1,512,256]{2,1,0:T(8,128)S(1)}, u32[]{:S(2)}, u32[]{:S(2)}) %collective-permute-start.8) | collective-permute-done | bytes 524320 | tf_op jit(solution)/shard_map/ppermute | solution.py:19
  154.1 4.2 %collective-permute-done.9 = f32[1,512,256]{2,1,0:T(8,128)} collective-permute-done((f32[1,512,256]{2,1,0:T(8,128)S(1)}, f32[1,512,256]{2,1,0:T(8,128)}, u32[]{:S(2)}, u32[]{:S(2)}) %collective-permute-start.9) | collective-permute-done | bytes 524320 | tf_op jit(solution)/shard_map/ppermute | solution.py:21
  158.2 7.2 %concatenate.65 = f32[1,3072,256]{2,1,0:T(8,128)S(1)} concatenate(f32[1,512,256]{2,1,0:T(8,128)} %copy-done.2, f32[1,1,256]{2,1,0:T(1,128)S(1)} %broadcast_select_fusion.3, f32[1,2047,256]{2,1,0:T(8,128)} %copy-done, f32[1,512,256]{2,1,0:T(8,128)} %collective-permute-done.9), dimensions={1} | concatenate | bytes 6291456 | tf_op jit(solution)/shard_map/concatenate | solution.py:17
  165.5 10.4 %multiply_add_fusion.3 = f32[1,2048,256]{2,1,0:T(8,128)S(1)} fusion(f32[1,3072,256]{2,1,0:T(8,128)S(1)} %concatenate.65, s32[]{:T(128)S(6)} %select_n.159, s32[]{:T(128)S(6)} %select_n.158, s32[]{:T(128)S(6)} %select_n.157, s32[]{:T(128)S(6)} %select_n.156, s32[]{:T(128)S(6)} %select_n.155, s32[]{:T(128)S(6)} %select_n.154, s32[]{:T(128)S(6)} %select_n.153, ...), kind=kLoop, calls=%fused_computation.27 | loop fusion | flops 12058624 | bytes 35651680 | tf_op jit(solution)/shard_map/add | solution.py:76
  179.5 13.4 %concatenate.66 = f32[2,2053,256]{2,1,0:T(8,128)} concatenate(f32[2,2,256]{2,1,0:T(2,128)S(1)} %broadcast.119, f32[2,2048,256]{2,1,0:T(8,128)} %pad_maximum_fusion, f32[2,1,256]{2,1,0:T(1,128)S(1)} %collective-permute-done.10, f32[2,2,256]{2,1,0:T(2,128)S(1)} %broadcast.119), dimensions={1} | concatenate | bytes 8409088 | tf_op jit(solution)/shard_map/concatenate | solution.py:36
  195.4 16.3 %copy.12 = f32[2,2052,256]{2,0,1:T(2,128)S(1)} copy(f32[2,2052,256]{2,1,0:T(8,128)S(1)} %constant_dynamic-slice_fusion.3) | data formatting | bytes 8404992 | tf_op jit(solution)/shard_map/dynamic_slice | solution.py:37
  211.7 4.2 %multiply_subtract_fusion.2 = (f32[2,1026,1,256]{3,0,2,1:T(2,128)S(1)}, f32[2,1026,1,256]{3,0,2,1:T(2,128)S(1)}) fusion(f32[2,1026,2,256]{3,0,2,1:T(2,128)S(1)} %bitcast.74, f32[1026]{0:T(1024)S(1)} %neg.21, f32[1026]{0:T(1024)S(1)} %get-tuple-element.65), kind=kLoop, calls=%fused_computation.26 | loop fusion | flops 3151872 | bytes 8413200 | tf_op jit(solution)/shard_map/sub | solution.py:42
  218.7 7.7 %fusion.7 = f32[1026]{0:T(1024)S(1)} fusion(f32[2,1026,2,256]{3,0,2,1:T(2,128)S(1)} %bitcast.75), kind=kLoop, calls=%fused_computation.59 | loop fusion | flops 1049598 | bytes 4206600 | tf_op jit(solution)/shard_map/reduce_sum | solution.py:50
  226.5 4.0 %collective-permute-start.12 = (f32[2,1,256]{2,0,1:T(2,128)S(1)}, f32[2,1,256]{2,0,1:T(2,128)S(1)}, u32[]{:S(2)}, u32[]{:S(2)}) collective-permute-start(f32[2,1,256]{2,0,1:T(2,128)S(1)} %get-tuple-element.19), channel_id=1, source_target_pairs={{0,28},{4,0},{8,4},{12,8},{16,12},{20,16},{24,20},{28,24},{1,29},{... | collective-permute-start | bytes 6152 | tf_op jit(solution)/shard_map/ppermute | solution.py:31
  233.4 4.2 %multiply_subtract_fusion.1 = (f32[2,1026,1,256]{3,0,2,1:T(2,128)S(1)}, f32[2,1026,1,256]{3,0,2,1:T(2,128)S(1)}) fusion(f32[2,1026,2,256]{3,0,2,1:T(2,128)S(1)} %bitcast.76, f32[1026]{0:T(1024)S(1)} %neg.22, f32[1026]{0:T(1024)S(1)} %get-tuple-element.62), kind=kLoop, calls=%fused_computation.24 | loop fusion | flops 3151872 | bytes 8413200 | tf_op jit(solution)/shard_map/sub | solution.py:42
  239.8 7.8 %fusion.6 = f32[1026]{0:T(1024)S(1)} fusion(f32[2,1026,2,256]{3,0,2,1:T(2,128)S(1)} %bitcast.77), kind=kLoop, calls=%fused_computation.58 | loop fusion | flops 1049598 | bytes 4206600 | tf_op jit(solution)/shard_map/reduce_sum | solution.py:50
  247.7 5.0 %collective-permute-start.14 = (f32[2,1,256]{2,0,1:T(2,128)S(1)}, f32[2,1,256]{2,0,1:T(2,128)S(1)}, u32[]{:S(2)}, u32[]{:S(2)}) collective-permute-start(f32[2,1,256]{2,0,1:T(2,128)S(1)} %get-tuple-element.17), channel_id=1, source_target_pairs={{0,28},{4,0},{8,4},{12,8},{16,12},{20,16},{24,20},{28,24},{1,29},{... | collective-permute-start | bytes 6152 | tf_op jit(solution)/shard_map/ppermute | solution.py:31
  255.5 4.2 %multiply_subtract_fusion = (f32[2,1026,1,256]{3,0,2,1:T(2,128)S(1)}, f32[2,1026,1,256]{3,0,2,1:T(2,128)S(1)}) fusion(f32[2,1026,2,256]{3,0,2,1:T(2,128)S(1)} %bitcast.78, f32[1026]{0:T(1024)S(1)} %neg.23, f32[1026]{0:T(1024)S(1)} %get-tuple-element.63), kind=kLoop, calls=%fused_computation.22 | loop fusion | flops 3151872 | bytes 8413200 | tf_op jit(solution)/shard_map/sub | solution.py:42
  261.7 7.7 %fusion.5 = f32[1026]{0:T(1024)S(1)} fusion(f32[2,1026,2,256]{3,0,2,1:T(2,128)S(1)} %bitcast.79), kind=kLoop, calls=%fused_computation.57 | loop fusion | flops 1049598 | bytes 4206600 | tf_op jit(solution)/shard_map/reduce_sum | solution.py:50
  269.6 5.0 %collective-permute-start.16 = (f32[2,1,256]{2,0,1:T(2,128)S(1)}, f32[2,1,256]{2,0,1:T(2,128)S(1)}, u32[]{:S(2)}, u32[]{:S(2)}) collective-permute-start(f32[2,1,256]{2,0,1:T(2,128)S(1)} %get-tuple-element.15), channel_id=1, source_target_pairs={{0,28},{4,0},{8,4},{12,8},{16,12},{20,16},{24,20},{28,24},{1,29},{... | collective-permute-start | bytes 6152 | tf_op jit(solution)/shard_map/ppermute | solution.py:31
  277.4 7.8 %fusion.4 = f32[1026]{0:T(1024)S(1)} fusion(f32[2,1026,2,256]{3,0,2,1:T(2,128)S(1)} %bitcast.89), kind=kLoop, calls=%fused_computation.56 | loop fusion | flops 1049598 | bytes 4206600 | tf_op jit(solution)/shard_map/reduce_sum | solution.py:50
  285.2 10.1 %all-reduce.7 = (f32[1,1024]{1,0:T(1,128)S(1)}, f32[1,1024]{1,0:T(1,128)S(1)}, f32[1,1024]{1,0:T(1,128)S(1)}, f32[1,1024]{1,0:T(1,128)S(1)}) all-reduce(f32[1,1024]{1,0:T(1,128)S(1)} %bitcast.102, f32[1,1024]{1,0:T(1,128)S(1)} %bitcast.103, f32[1,1024]{1,0:T(1,128)S(1)} %bitcast.104, ...), channel_id=1, replica_groups=mesh['blk'=8,'col'=4] {'col'}, use_global_device_ids=true, to_apply=%region_7.8 | all-reduce | flops 4096 | bytes 32768 | tf_op jit(solution)/shard_map/psum | solution.py:97
  (120 shorter events, 66.2 us)
Async XLA Ops:
  1.3 48.4 %collective-permute-start = (f32[1,1,256]{2,1,0:T(1,128)S(1)}, f32[1,1,256]{2,1,0:T(1,128)S(1)}, u32[]{:S(2)}, u32[]{:S(2)}) collective-permute-start(f32[1,1,256]{2,1,0:T(1,128)S(1)} %slice.421), channel_id=1, source_target_pairs={{0,28},{4,0},{8,4},{12,8},{16,12},{20,16},{24,20},{28,24},{1,29},{... | collective-permute-start | bytes 3080 | tf_op jit(solution)/shard_map/ppermute | solution.py:31
  71.7 6.3 %collective-permute-start.1 = (f32[1,1,256]{2,0,1:T(1,128)S(1)}, f32[1,1,256]{2,0,1:T(1,128)S(1)}, u32[]{:S(2)}, u32[]{:S(2)}) collective-permute-start(f32[1,1,256]{2,0,1:T(1,128)S(1)} %pad_dynamic-slice_fusion.15), channel_id=1, source_target_pairs={{0,4},{4,8},{8,12},{12,16},{16,20},{20,24},{24,28},{28,0},{1,5},{5... | collective-permute-start | bytes 3080 | tf_op jit(solution)/shard_map/ppermute | solution.py:31
  78.6 3.6 %collective-permute-start.2 = (f32[1,1,256]{2,0,1:T(1,128)S(1)}, f32[1,1,256]{2,0,1:T(1,128)S(1)}, u32[]{:S(2)}, u32[]{:S(2)}) collective-permute-start(f32[1,1,256]{2,0,1:T(1,128)S(1)} %get-tuple-element.25), channel_id=1, source_target_pairs={{0,28},{4,0},{8,4},{12,8},{16,12},{20,16},{24,20},{28,24},{1,29},{... | collective-permute-start | bytes 3080 | tf_op jit(solution)/shard_map/ppermute | solution.py:31
  92.5 6.3 %collective-permute-start.3 = (f32[1,1,256]{2,0,1:T(1,128)S(1)}, f32[1,1,256]{2,0,1:T(1,128)S(1)}, u32[]{:S(2)}, u32[]{:S(2)}) collective-permute-start(f32[1,1,256]{2,0,1:T(1,128)S(1)} %pad_dynamic-slice_fusion.13), channel_id=1, source_target_pairs={{0,4},{4,8},{8,12},{12,16},{16,20},{20,24},{24,28},{28,0},{1,5},{5... | collective-permute-start | bytes 3080 | tf_op jit(solution)/shard_map/ppermute | solution.py:31
  99.4 3.6 %collective-permute-start.4 = (f32[1,1,256]{2,0,1:T(1,128)S(1)}, f32[1,1,256]{2,0,1:T(1,128)S(1)}, u32[]{:S(2)}, u32[]{:S(2)}) collective-permute-start(f32[1,1,256]{2,0,1:T(1,128)S(1)} %get-tuple-element.23), channel_id=1, source_target_pairs={{0,28},{4,0},{8,4},{12,8},{16,12},{20,16},{24,20},{28,24},{1,29},{... | collective-permute-start | bytes 3080 | tf_op jit(solution)/shard_map/ppermute | solution.py:31
  113.3 6.3 %collective-permute-start.5 = (f32[1,1,256]{2,0,1:T(1,128)S(1)}, f32[1,1,256]{2,0,1:T(1,128)S(1)}, u32[]{:S(2)}, u32[]{:S(2)}) collective-permute-start(f32[1,1,256]{2,0,1:T(1,128)S(1)} %pad_dynamic-slice_fusion.11), channel_id=1, source_target_pairs={{0,4},{4,8},{8,12},{12,16},{16,20},{20,24},{24,28},{28,0},{1,5},{5... | collective-permute-start | bytes 3080 | tf_op jit(solution)/shard_map/ppermute | solution.py:31
  120.2 3.6 %collective-permute-start.6 = (f32[1,1,256]{2,0,1:T(1,128)S(1)}, f32[1,1,256]{2,0,1:T(1,128)S(1)}, u32[]{:S(2)}, u32[]{:S(2)}) collective-permute-start(f32[1,1,256]{2,0,1:T(1,128)S(1)} %get-tuple-element.21), channel_id=1, source_target_pairs={{0,28},{4,0},{8,4},{12,8},{16,12},{20,16},{24,20},{28,24},{1,29},{... | collective-permute-start | bytes 3080 | tf_op jit(solution)/shard_map/ppermute | solution.py:31
  134.6 13.3 %copy-start = (f32[1,2047,256]{2,1,0:T(8,128)}, f32[1,2047,256]{2,1,0:T(8,128)S(1)}, u32[]{:S(2)}) copy-start(f32[1,2047,256]{2,1,0:T(8,128)S(1)} %pad_dynamic-slice_fusion.6) | copy-start | bytes 6288388
  134.7 6.5 %collective-permute-start.7 = (f32[1,1,256]{2,1,0:T(1,128)S(1)}, f32[1,1,256]{2,1,0:T(1,128)S(1)}, u32[]{:S(2)}, u32[]{:S(2)}) collective-permute-start(f32[1,1,256]{2,1,0:T(1,128)S(1)} %pad_dynamic-slice_fusion.8), channel_id=1, source_target_pairs={{0,4},{4,8},{8,12},{12,16},{16,20},{20,24},{24,28},{28,0},{1,5},{5... | collective-permute-start | bytes 3080 | tf_op jit(solution)/shard_map/ppermute | solution.py:31
  136.0 17.2 %collective-permute-start.8 = (f32[1,512,256]{2,1,0:T(8,128)S(1)}, f32[1,512,256]{2,1,0:T(8,128)S(1)}, u32[]{:S(2)}, u32[]{:S(2)}) collective-permute-start(f32[1,512,256]{2,1,0:T(8,128)S(1)} %pad_dynamic-slice_fusion.9), channel_id=1, source_target_pairs={{0,4},{4,8},{8,12},{12,16},{16,20},{20,24},{24,28},{28,0},{1,5},{5... | collective-permute-start | bytes 1572872 | tf_op jit(solution)/shard_map/ppermute | solution.py:19
  141.2 17.0 %collective-permute-start.9 = (f32[1,512,256]{2,1,0:T(8,128)S(1)}, f32[1,512,256]{2,1,0:T(8,128)}, u32[]{:S(2)}, u32[]{:S(2)}) collective-permute-start(f32[1,512,256]{2,1,0:T(8,128)S(1)} %fusion.8), channel_id=1, source_target_pairs={{4,0},{8,4},{12,8},{16,12},{20,16},{24,20},{28,24},{0,28},{5,1},{9... | collective-permute-start | bytes 1572872 | tf_op jit(solution)/shard_map/ppermute | solution.py:21
  153.3 0.8 copy-start.2
  165.5 10.4 %copy-start.1 = (f32[1,2048,256]{2,1,0:T(8,128)S(1)}, f32[1,2048,256]{2,1,0:T(8,128)}, u32[]{:S(2)}) copy-start(f32[1,2048,256]{2,1,0:T(8,128)} %pad_maximum_fusion.4) | copy-start | bytes 6291460
  175.9 3.6 %collective-permute-start.10 = (f32[2,1,256]{2,1,0:T(1,128)S(1)}, f32[2,1,256]{2,1,0:T(1,128)S(1)}, u32[]{:S(2)}, u32[]{:S(2)}) collective-permute-start(f32[2,1,256]{2,1,0:T(1,128)S(1)} %fusion.9), channel_id=1, source_target_pairs={{0,28},{4,0},{8,4},{12,8},{16,12},{20,16},{24,20},{28,24},{1,29},{... | collective-permute-start | bytes 6152 | tf_op jit(solution)/shard_map/ppermute | solution.py:31
  215.9 10.6 %slice-start.4 = ((s8[4204544]{0:T(1024)(128)(4,1)}), s8[4194304]{0:T(1024)(128)(4,1)S(1)}, s32[]{:S(2)}) async-start(s8[4204544]{0:T(1024)(128)(4,1)} %bitcast.98), calls=%async_computation.4 | async-start | bytes 8388608
  217.9 8.6 %slice-start.5 = ((s8[4204544]{0:T(1024)(128)(4,1)}), s8[10240]{0:T(1024)(128)(4,1)S(1)}, s32[]{:S(2)}) async-start(s8[4204544]{0:T(1024)(128)(4,1)} %bitcast.98), calls=%async_computation.5 | async-start | bytes 20480
  217.9 8.6 %collective-permute-start.11 = (f32[2,1,256]{2,0,1:T(2,128)S(1)}, f32[2,1,256]{2,0,1:T(2,128)S(1)}, u32[]{:S(2)}, u32[]{:S(2)}) collective-permute-start(f32[2,1,256]{2,0,1:T(2,128)S(1)} %pad_dynamic-slice_fusion.5), channel_id=1, source_target_pairs={{0,4},{4,8},{8,12},{12,16},{16,20},{20,24},{24,28},{28,0},{1,5},{5... | collective-permute-start | bytes 6152 | tf_op jit(solution)/shard_map/ppermute | solution.py:31
  226.5 5.3 %collective-permute-start.12 = (f32[2,1,256]{2,0,1:T(2,128)S(1)}, f32[2,1,256]{2,0,1:T(2,128)S(1)}, u32[]{:S(2)}, u32[]{:S(2)}) collective-permute-start(f32[2,1,256]{2,0,1:T(2,128)S(1)} %get-tuple-element.19), channel_id=1, source_target_pairs={{0,28},{4,0},{8,4},{12,8},{16,12},{20,16},{24,20},{28,24},{1,29},{... | collective-permute-start | bytes 6152 | tf_op jit(solution)/shard_map/ppermute | solution.py:31
  237.5 10.1 %slice-start.2 = ((s8[4204544]{0:T(1024)(128)(4,1)}), s8[4194304]{0:T(1024)(128)(4,1)S(1)}, s32[]{:S(2)}) async-start(s8[4204544]{0:T(1024)(128)(4,1)} %bitcast.96), calls=%async_computation.2 | async-start | bytes 8388608
  239.5 8.2 %slice-start.3 = ((s8[4204544]{0:T(1024)(128)(4,1)}), s8[10240]{0:T(1024)(128)(4,1)S(1)}, s32[]{:S(2)}) async-start(s8[4204544]{0:T(1024)(128)(4,1)} %bitcast.96), calls=%async_computation.3 | async-start | bytes 20480
  239.5 8.1 %collective-permute-start.13 = (f32[2,1,256]{2,0,1:T(2,128)S(1)}, f32[2,1,256]{2,0,1:T(2,128)S(1)}, u32[]{:S(2)}, u32[]{:S(2)}) collective-permute-start(f32[2,1,256]{2,0,1:T(2,128)S(1)} %pad_dynamic-slice_fusion.3), channel_id=1, source_target_pairs={{0,4},{4,8},{8,12},{12,16},{16,20},{20,24},{24,28},{28,0},{1,5},{5... | collective-permute-start | bytes 6152 | tf_op jit(solution)/shard_map/ppermute | solution.py:31
  247.7 6.3 %collective-permute-start.14 = (f32[2,1,256]{2,0,1:T(2,128)S(1)}, f32[2,1,256]{2,0,1:T(2,128)S(1)}, u32[]{:S(2)}, u32[]{:S(2)}) collective-permute-start(f32[2,1,256]{2,0,1:T(2,128)S(1)} %get-tuple-element.17), channel_id=1, source_target_pairs={{0,28},{4,0},{8,4},{12,8},{16,12},{20,16},{24,20},{28,24},{1,29},{... | collective-permute-start | bytes 6152 | tf_op jit(solution)/shard_map/ppermute | solution.py:31
  259.7 9.8 %slice-start = ((s8[4204544]{0:T(1024)(128)(4,1)}), s8[4194304]{0:T(1024)(128)(4,1)S(1)}, s32[]{:S(2)}) async-start(s8[4204544]{0:T(1024)(128)(4,1)} %bitcast.94), calls=%async_computation | async-start | bytes 8388608
  261.6 7.9 %slice-start.1 = ((s8[4204544]{0:T(1024)(128)(4,1)}), s8[10240]{0:T(1024)(128)(4,1)S(1)}, s32[]{:S(2)}) async-start(s8[4204544]{0:T(1024)(128)(4,1)} %bitcast.94), calls=%async_computation.1 | async-start | bytes 20480
  261.7 7.9 %collective-permute-start.15 = (f32[2,1,256]{2,0,1:T(2,128)S(1)}, f32[2,1,256]{2,0,1:T(2,128)S(1)}, u32[]{:S(2)}, u32[]{:S(2)}) collective-permute-start(f32[2,1,256]{2,0,1:T(2,128)S(1)} %pad_dynamic-slice_fusion.1), channel_id=1, source_target_pairs={{0,4},{4,8},{8,12},{12,16},{16,20},{20,24},{24,28},{28,0},{1,5},{5... | collective-permute-start | bytes 6152 | tf_op jit(solution)/shard_map/ppermute | solution.py:31
  269.6 6.3 %collective-permute-start.16 = (f32[2,1,256]{2,0,1:T(2,128)S(1)}, f32[2,1,256]{2,0,1:T(2,128)S(1)}, u32[]{:S(2)}, u32[]{:S(2)}) collective-permute-start(f32[2,1,256]{2,0,1:T(2,128)S(1)} %get-tuple-element.15), channel_id=1, source_target_pairs={{0,28},{4,0},{8,4},{12,8},{16,12},{20,16},{24,20},{28,24},{1,29},{... | collective-permute-start | bytes 6152 | tf_op jit(solution)/shard_map/ppermute | solution.py:31
where the time goes:
time: 298 us; the launch traced here: 296 us
  local copies, waits for them, and re-layouts  93.6 us (31%)
  other arithmetic  93.5 us (31%)
  between operations  36.3 us (12%)
  waiting for transfers between devices  31.7 us (11%)
  starting transfers between devices  30.8 us (10%)
  blocking collectives  10.1 us (3%)
    dynamic_slice x9, local copies, waits for them, and re-layouts, rotate_frame(): lax.dynamic_slice_in_dim(padded, offset, rows, 1)  34.8 us
    sub x7, other arithmetic, rotate_frame(): new_first = cos_b * first - sin_b * second  31 us
    reduce_sum x4, other arithmetic, pair_gradient(): whole = jnp.sum(second[0] * first[1] - first[0] * second[1], axis=1)  31 us
    ppermute x15, starting transfers between devices, shifted(): return lax.ppermute(value, axis, pairs)  25.4 us
    ppermute x15, waiting for transfers between devices, shifted(): return lax.ppermute(value, axis, pairs)  23.7 us
    concatenate x8, local copies, waits for them, and re-layouts, rotate_frame(): jnp.concatenate([stack, jnp.zeros((fields, 1, width), stack.dtype)], 1)  23.3 us
    unnamed x36, local copies, waits for them, and re-layouts  17.3 us
    another operation x7, other arithmetic, rotate_frame(): flat = jnp.stack([new_first, new_second], 2).reshape(fields, rows, width)  13.4 us
  transfers between devices with their start and end apart: 17, of which 13 were waited for; matrix products, arithmetic and copies ran while one was open for 17% of the time, Pallas kernels for 0%

commit v1 on v0

v1 whole, which is shorter than its diff:
```python
import functools

import jax
import jax.numpy as jnp
from jax import lax
from jax.experimental import pallas as pl
from jax.experimental.pallas import tpu as pltpu
from jax.sharding import PartitionSpec as P

LAYERS = 4
BANDS = 8
REACH = 512
HALF = REACH // 2
SENT = HALF + 8
LANES = 128
FRONT = SENT + 8
STEP = 48
MESH = pl.DeviceIdType.MESH


def sweep(low, high, step, body):
    assert (high - low) % step == 0 and low % 8 == 0 and step % 8 == 0

    def one(i, carry):
        body(pl.multiple_of(low + i * step, 8))
        return carry

    lax.fori_loop(0, (high - low) // step, one, 0)


def kernel(
    nblk, ncol,
    pairing, offsets, weights, slab, angles,
    out, grad,
    raw, land, angw, coef, sa, sb, field, adj, xa, xb, prod, stage, window,
    own_g, left_g, right_g, send_l, send_r,
    load_sem, ang_sem, out_sem, h_send, h_recv, a_send, a_recv, o_send, o_recv, l_send, l_recv, r_send, r_recv,
):
    rows, width = slab.shape
    halves = width // LANES
    pairs = rows // 2
    q_own = HALF
    q_end = q_own + pairs
    q_lo, q_hi = 120, q_end + 136
    total_q = pairs + REACH
    blk = lax.axis_index("blk")
    col = lax.axis_index("col")
    after = lax.rem(blk + 1, nblk)
    before = lax.rem(blk + nblk - 1, nblk)
    others = [lax.rem(col + d, ncol) for d in range(1, ncol)]
    every = [col] + others

    barrier = pltpu.get_barrier_semaphore()
    peers = [(blk, c) for c in others] + [(b, c) for b in (after, before) for c in every]
    for peer in peers:
        pl.semaphore_signal(barrier, inc=1, device_id=peer, device_id_type=MESH)

    loads = []
    for h in range(halves):
        loads.append(pltpu.make_async_copy(
            slab.at[:, pl.ds(h * LANES, LANES)], raw.at[h, pl.ds(FRONT, rows)], load_sem.at[h]))
    own_ang = pltpu.make_async_copy(angles, angw.at[:, pl.ds(HALF, pairs)], ang_sem)
    own_ang.start()
    for load in loads:
        load.start()

    def remote(src, dst, s, r, peer):
        return pltpu.make_async_remote_copy(
            src_ref=src, dst_ref=dst, send_sem=s, recv_sem=r, device_id=peer, device_id_type=MESH)

    ang_copies = [
        remote(angles.at[:, pl.ds(pairs - HALF, HALF)], angw.at[:, pl.ds(0, HALF)], a_send.at[0], a_recv.at[0], (after, col)),
        remote(angles.at[:, pl.ds(0, HALF)], angw.at[:, pl.ds(q_end, HALF)], a_send.at[1], a_recv.at[1], (before, col)),
    ]
    halo_copies = []
    for h in range(halves):
        lanes = pl.ds(h * LANES, LANES)
        halo_copies.append([
            remote(slab.at[pl.ds(rows - SENT, SENT), lanes], land.at[h, 0], h_send.at[h, 0], h_recv.at[h, 0], (after, col)),
            remote(slab.at[pl.ds(0, SENT), lanes], land.at[h, 1], h_send.at[h, 1], h_recv.at[h, 1], (before, col)),
        ])

    pl.semaphore_wait(barrier, len(peers))
    for copy in ang_copies:
        copy.start()
    for pair in halo_copies:
        for copy in pair:
            copy.start()

    first = pairing[0]

    def zeros(n):
        return jnp.zeros((n, LANES), jnp.float32)

    for h in range(halves):
        raw[h, 0:8, :] = zeros(8)
        raw[h, FRONT + rows + SENT:FRONT + rows + SENT + 16, :] = zeros(16)
        adj[h, 2 * q_lo:REACH - HALF, :] = zeros(REACH - HALF - 2 * q_lo)
        top = REACH + rows + HALF
        adj[h, top:2 * q_hi + 8, :] = zeros(2 * q_hi + 8 - top)
        field[h, 0:2 * q_lo + 8, :] = zeros(2 * q_lo + 8)
        field[h, 2 * q_hi:, :] = zeros(field.shape[1] - 2 * q_hi)
        for l in range(LAYERS):
            sa[h, l, q_hi:q_hi + 8, :] = zeros(8)
            sb[h, l, q_lo - 8:q_lo, :] = zeros(8)
            prod[h, l, 0:q_lo, :] = zeros(q_lo)
            prod[h, l, q_hi:total_q, :] = zeros(total_q - q_hi)
        for l in range(LAYERS - 1):
            xb[h, l, q_lo - 8:q_lo, :] = zeros(8)
            xa[h, l, q_hi:q_hi + 8, :] = zeros(8)

    own_ang.wait()
    for copy in ang_copies:
        copy.wait()
    theta = angw[...]
    both = jnp.concatenate([jnp.cos(theta), jnp.sin(theta)], 0)
    rolled = pltpu.roll(both, total_q - 1, 1)
    odd = lax.broadcasted_iota(jnp.int32, both.shape, 0) % 2 == 1
    moved = jnp.full(both.shape, first, jnp.int32) == 1
    window[...] = jnp.where(jnp.logical_and(odd, moved), rolled, both)

    def spread(q):
        part = window[:, pl.ds(pl.multiple_of(q, LANES), LANES)]
        turned = part.T
        for j in range(2 * LAYERS):
            coef[j, pl.ds(q, LANES), :] = jnp.broadcast_to(turned[:, j:j + 1], (LANES, LANES))

    sweep(0, total_q, LANES, spread)

    def forward(h, low, high, step):
        for l in range(LAYERS):
            def body(q, l=l):
                if l == 0:
                    a = raw[h, pl.ds(2 * q - 2 * q_lo + first, step, stride=2), :]
                    b = raw[h, pl.ds(2 * q - 2 * q_lo + 1 + first, step, stride=2), :]
                elif l % 2 == 1:
                    a = sb[h, l - 1, pl.ds(q, step), :]
                    b = sa[h, l - 1, pl.ds(q + 1, step), :]
                else:
                    a = sb[h, l - 1, pl.ds(q - 1, step), :]
                    b = sa[h, l - 1, pl.ds(q, step), :]
                c = coef[l, pl.ds(q, step), :]
                s = coef[LAYERS + l, pl.ds(q, step), :]
                new_a = c * a - s * b
                new_b = s * a + c * b
                sa[h, l, pl.ds(q, step), :] = new_a
                sb[h, l, pl.ds(q, step), :] = new_b
                if l == LAYERS - 1:
                    field[h, pl.ds(2 * q + 1, step, stride=2), :] = new_a
                    field[h, pl.ds(2 * q + 2, step, stride=2), :] = new_b
            sweep(low, high, step, body)

    def emit(h, low, high):
        def body(r):
            stage[h, pl.ds(r, 64), :] = field[h, pl.ds(r + REACH - first, 64), :]
        sweep(low, high, 64, body)
        return pltpu.make_async_copy(
            stage.at[h, pl.ds(low, high - low)],
            out.at[pl.ds(low, high - low), pl.ds(h * LANES, LANES)],
            out_sem.at[h, 0 if low == 64 else (1 if low == 0 else 2)])

    reach = [offsets[k] for k in range(BANDS)]
    weight = [weights[k] for k in range(BANDS)]

    def band(h, low, high, upper=True, lower=True, up_from=None, up_to=None, down_from=None, down_to=None):
        n = 64

        def body(t):
            acc = jnp.zeros((n, LANES), jnp.float32)
            spot = lax.broadcasted_iota(jnp.int32, (n, LANES), 0)
            for k in range(BANDS):
                part = None
                if upper:
                    at = t + reach[k]
                    part = field[h, pl.ds(at, n), :]
                    if up_from is not None:
                        part = jnp.where(spot >= up_from + REACH - at, part, 0.0)
                    if up_to is not None:
                        part = jnp.where(spot < up_to + REACH - at, part, 0.0)
                if lower:
                    at = t - reach[k]
                    down = field[h, pl.ds(at, n), :]
                    if down_from is not None:
                        down = jnp.where(spot >= down_from + REACH - at, down, 0.0)
                    if down_to is not None:
                        down = jnp.where(spot < down_to + REACH - at, down, 0.0)
                    part = down if part is None else part + down
                acc = acc + weight[k] * part
            adj[h, pl.ds(t, n), :] = acc
        sweep(low + REACH, high + REACH, n, body)

    def backward(h, low, high, step):
        for l in reversed(range(LAYERS)):
            def body(q, l=l):
                if l == LAYERS - 1:
                    a = adj[h, pl.ds(2 * q + 1, step, stride=2), :]
                    b = adj[h, pl.ds(2 * q + 2, step, stride=2), :]
                elif l % 2 == 1:
                    a = xb[h, l, pl.ds(q, step), :]
                    b = xa[h, l, pl.ds(q + 1, step), :]
                else:
                    a = xb[h, l, pl.ds(q - 1, step), :]
                    b = xa[h, l, pl.ds(q, step), :]
                prod[h, l, pl.ds(q, step), :] = b * sa[h, l, pl.ds(q, step), :] - a * sb[h, l, pl.ds(q, step), :]
                if l > 0:
                    c = coef[l, pl.ds(q, step), :]
                    s = coef[LAYERS + l, pl.ds(q, step), :]
                    xa[h, l - 1, pl.ds(q, step), :] = c * a + s * b
                    xb[h, l - 1, pl.ds(q, step), :] = c * b - s * a
            sweep(low, high, step, body)

    outs = []
    for load in loads:
        load.wait()
    for h in range(halves):
        forward(h, q_own, q_end - 16, STEP)
        outs.append(emit(h, 64, rows - 64))
        outs[-1].start()
        band(h, REACH + 16, rows - REACH - 48)
        backward(h, q_own + 264, q_end - 280, STEP)

    for h in range(halves):
        for copy in halo_copies[h]:
            copy.wait()
        raw[h, 8:8 + SENT, :] = land[h, 0]
        raw[h, FRONT + rows:FRONT + rows + SENT, :] = land[h, 1]
        forward(h, q_lo, q_own + 8, STEP)
        forward(h, q_end - 24, q_hi, 40)
        for low, high in ((0, 64), (rows - 64, rows)):
            outs.append(emit(h, low, high))
            outs[-1].start()
        band(h, -HALF, 0, lower=False, up_from=0)
        band(h, 0, REACH + 64, down_from=-HALF)
        band(h, rows - REACH - 64, rows - HALF)
        band(h, rows - HALF, rows, up_to=rows)
        band(h, rows, rows + HALF, upper=False, down_to=rows - HALF)
        backward(h, q_lo, q_lo + 432, STEP)
        backward(h, q_hi - 432, q_hi, STEP)

    diagonal = (lax.broadcasted_iota(jnp.int32, (LANES, LANES), 0)
                == lax.broadcasted_iota(jnp.int32, (LANES, LANES), 1))

    def collapse(q):
        for l in range(LAYERS):
            x = prod[0, l, pl.ds(q, LANES), :]
            for h in range(1, halves):
                x = x + prod[h, l, pl.ds(q, LANES), :]
            s = jnp.sum(x, axis=1, keepdims=True)
            line = jnp.sum(jnp.where(diagonal, s, 0.0), axis=0, keepdims=True)
            window[l:l + 1, pl.ds(pl.multiple_of(q, LANES), LANES)] = line

    sweep(0, total_q, LANES, collapse)
    whole = window[...]
    rolled = pltpu.roll(whole, 1, 1)
    whole = jnp.where(jnp.logical_and(odd, moved), rolled, whole)[:LAYERS]
    mid = q_own + pairs // 2
    own_g[pl.ds(col, 1)] = jnp.concatenate([whole[:, q_own:mid], whole[:, mid:q_end]], 0)[None]
    send_l[...] = jnp.concatenate([whole[:, 0:LANES], whole[:, LANES:HALF]], 0)
    send_r[...] = jnp.concatenate([whole[:, q_end:q_end + LANES], whole[:, q_end + LANES:]], 0)
    copies = []
    for i, c in enumerate(others):
        copies.append(remote(own_g.at[col], own_g.at[col], o_send.at[i], o_recv.at[col], (blk, c)))
    for i, c in enumerate(every):
        copies.append(remote(send_l, right_g.at[col], l_send.at[i], l_recv.at[col], (before, c)))
        copies.append(remote(send_r, left_g.at[col], r_send.at[i], r_recv.at[col], (after, c)))
    for copy in copies:
        copy.start()
    for copy in copies:
        copy.wait_send()
    for i, c in enumerate(others):
        remote(own_g.at[c], own_g.at[c], o_send.at[i], o_recv.at[c], (blk, c)).wait_recv()
    for i, c in enumerate(every):
        remote(send_l, right_g.at[c], l_send.at[i], l_recv.at[c], (before, c)).wait_recv()
        remote(send_r, left_g.at[c], r_send.at[i], r_recv.at[c], (after, c)).wait_recv()
    own = own_g[0]
    left = left_g[0]
    right = right_g[0]
    for c in range(1, ncol):
        own = own + own_g[c]
        left = left + left_g[c]
        right = right + right_g[c]
    line = jnp.concatenate([own[:LAYERS], own[LAYERS:]], 1)
    line = jnp.concatenate([
        line[:, :LANES] + left[:LAYERS],
        line[:, LANES:HALF] + left[LAYERS:],
        line[:, HALF:pairs - HALF],
        line[:, pairs - HALF:pairs - LANES] + right[:LAYERS],
        line[:, pairs - LANES:] + right[LAYERS:],
    ], 1)
    grad[...] = line
    for copy in outs:
        copy.wait()


def on_device(nblk, ncol, slab, angles, pairing, band_offsets, band_weights):
    rows, width = slab.shape
    halves = width // LANES
    pairs = rows // 2
    total_q = pairs + REACH
    buf_q = total_q + 8
    f32 = jnp.float32
    dma = pltpu.SemaphoreType.DMA
    smem = pl.BlockSpec(memory_space=pltpu.SMEM)
    anywhere = pl.BlockSpec(memory_space=pl.ANY)
    return pl.pallas_call(
        functools.partial(kernel, nblk, ncol),
        out_shape=(
            jax.ShapeDtypeStruct((rows, width), f32),
            jax.ShapeDtypeStruct((LAYERS, pairs), f32),
        ),
        in_specs=[smem, smem, smem, anywhere, anywhere],
        out_specs=(anywhere, pl.BlockSpec(memory_space=pltpu.VMEM)),
        scratch_shapes=[
            pltpu.VMEM((halves, FRONT + rows + SENT + 16, LANES), f32),
            pltpu.VMEM((halves, 2, SENT, LANES), f32),
            pltpu.VMEM((LAYERS, total_q), f32),
            pltpu.VMEM((2 * LAYERS, total_q, LANES), f32),
            pltpu.VMEM((halves, LAYERS, buf_q, LANES), f32),
            pltpu.VMEM((halves, LAYERS, buf_q, LANES), f32),
            pltpu.VMEM((halves, rows + 2 * REACH + 16, LANES), f32),
            pltpu.VMEM((halves, rows + 2 * REACH + 16, LANES), f32),
            pltpu.VMEM((halves, LAYERS - 1, buf_q, LANES), f32),
            pltpu.VMEM((halves, LAYERS - 1, buf_q, LANES), f32),
            pltpu.VMEM((halves, LAYERS, total_q, LANES), f32),
            pltpu.VMEM((halves, rows, LANES), f32),
            pltpu.VMEM((2 * LAYERS, total_q), f32),
            pltpu.VMEM((ncol, 2 * LAYERS, pairs // 2), f32),
            pltpu.VMEM((ncol, 2 * LAYERS, LANES), f32),
            pltpu.VMEM((ncol, 2 * LAYERS, LANES), f32),
            pltpu.VMEM((2 * LAYERS, LANES), f32),
            pltpu.VMEM((2 * LAYERS, LANES), f32),
            dma((halves,)), dma, dma((halves, 3)),
            dma((halves, 2)), dma((halves, 2)),
            dma((2,)), dma((2,)),
            dma((ncol - 1,)), dma((ncol,)),
            dma((ncol,)), dma((ncol,)),
            dma((ncol,)), dma((ncol,)),
        ],
        compiler_params=pltpu.CompilerParams(
            collective_id=0, has_side_effects=True, vmem_limit_bytes=58 * 2**20),
    )(pairing, band_offsets, band_weights, slab, angles)


def solution(mesh):
    in_specs = (P("blk", "col"), P(None, "blk"), P(), P(), P())
    out_specs = (P("blk", "col"), P(None, "blk"))
    return jax.shard_map(
        functools.partial(on_device, mesh.shape["blk"], mesh.shape["col"]),
        mesh=mesh, in_specs=in_specs, out_specs=out_specs, check_vma=False,
    )
```

time: 298 us -> 37.8 us (0.13)
  other arithmetic: 93.5 us -> 0 us
  local copies, waits for them, and re-layouts: 93.6 us -> 3.66 us
  between operations: 36.3 us -> 0.65 us
  Pallas kernels: 0 us -> 33.3 us
  waiting for transfers between devices: 31.7 us -> 0 us
  starting transfers between devices: 30.8 us -> 0 us
  blocking collectives: 10.1 us -> 0 us
    dynamic_slice x9 -> x0, local copies, waits for them, and re-layouts: 34.8 us -> none  [rotate_frame(): lax.dynamic_slice_in_dim(padded, offset, rows, 1)]
    pallas_call x0 -> x1, Pallas kernels: none -> 33.3 us  [on_device(): pl.pallas_call(functools.partial(kernel, nblk, ncol), out_shape=(jax.Shap...]
    ppermute x17 -> x0, waiting for transfers between devices: 31.7 us -> none  [the longest x15 23.7 us: shifted(): return lax.ppermute(value, axis, pairs)]
    concatenate x10 -> x0, local copies, waits for them, and re-layouts: 31.3 us -> none  [the longest x8 23.3 us: rotate_frame(): jnp.concatenate([stack, jnp.zeros((fields, 1, width), stack.dtype)], 1)]
    sub x7 -> x0, other arithmetic: 31 us -> none  [rotate_frame(): new_first = cos_b * first - sin_b * second]
    reduce_sum x4 -> x0, other arithmetic: 31 us -> none  [pair_gradient(): whole = jnp.sum(second[0] * first[1] - first[0] * second[1], axis=1)]
    ppermute x17 -> x0, starting transfers between devices: 30.8 us -> none  [the longest x15 25.4 us: shifted(): return lax.ppermute(value, axis, pairs)]
    another operation x10 -> x0, other arithmetic: 16.4 us -> none  [the longest x7 13.4 us: rotate_frame(): flat = jnp.stack([new_first, new_second], 2).reshape(fields, rows, width)]
  transfers between devices with their start and end apart: 17 -> 0, of which waited for: 13 -> 0; matrix products, arithmetic and copies ran while one was open for 17% -> 0% of each run, Pallas kernels for 0% -> 0%
where the time goes in v1:
time: 37.8 us; the launch traced here: 37.6 us
  Pallas kernels  33.3 us (88%)
  local copies, waits for them, and re-layouts  3.66 us (10%)
  between operations  0.65 us (2%)
    pallas_call x1, Pallas kernels, on_device(): pl.pallas_call(functools.partial(kernel, nblk, ncol), out_shape=(jax.Shap...  33.3 us
    unnamed x4, local copies, waits for them, and re-layouts  3.66 us

profile of v1, /device:TPU:0, one launch (start us, length us, event | category | flops | bytes accessed | tf_op | source)
XLA Modules:
  0.0 37.6 jit_solution(16044164301387773383)
XLA Ops:
  0.6 33.3 %shard_map.68 = (f32[2048,256]{1,0:T(8,128)}, f32[4,1024]{1,0:T(4,128)}) custom-call(s32[4]{0:T(128)} %pairing.1, s32[8]{0:T(128)} %offsets.1, f32[8]{0:T(128)} %weights.1, f32[2048,256]{1,0:T(8,128)} %slab.1, f32[4,1024]{1,0:T(4,128)} %angles.1), custom_call_target="tpu_custom_call" | custom-call | tf_op jit(solution)/shard_map/pallas_call | solution.py:305
  33.9 0.0 copy-start
  34.0 3.0 %copy.9 = f32[2048,256]{1,0:T(8,128)} copy(f32[2048,256]{1,0:T(8,128)} %get-tuple-element.4) | data formatting | bytes 4194304
  37.0 0.0 copy-done
  37.0 0.6 %copy.10 = f32[4,1024]{1,0:T(4,128)} copy(f32[4,1024]{1,0:T(4,128)S(1)} %copy-done) | data formatting | bytes 32768
Async XLA Ops:
  33.9 3.1 %copy-start = (f32[4,1024]{1,0:T(4,128)S(1)}, f32[4,1024]{1,0:T(4,128)}, u32[]{:S(2)}) copy-start(f32[4,1024]{1,0:T(4,128)} %get-tuple-element.5) | copy-start | bytes 49156

commit v2 on v1

--- a/solution.py
+++ b/solution.py
@@ -14,27 +14,41 @@
 SENT = HALF + 8
 LANES = 128
 FRONT = SENT + 8
-STEP = 48
 MESH = pl.DeviceIdType.MESH
 
 
 def sweep(low, high, step, body):
     assert (high - low) % step == 0 and low % 8 == 0 and step % 8 == 0
+    if high - low == step:
+        body(low)
+        return
 
     def one(i, carry):
         body(pl.multiple_of(low + i * step, 8))
         return carry
 
     lax.fori_loop(0, (high - low) // step, one, 0)
+
+
+def sin_cos(x):
+    n = jnp.floor(x * 0.6366197723675814 + 0.5)
+    r = ((x - n * 1.5703125) - n * 4.837512969970703e-4) - n * 7.54978995489188e-8
+    z = r * r
+    s = ((-1.9515295891e-4 * z + 8.3321608736e-3) * z - 1.6666654611e-1) * z * r + r
+    c = ((2.443315711809948e-5 * z - 1.388731625493765e-3) * z + 4.166664568298827e-2) * z * z - 0.5 * z + 1.0
+    odd = jnp.abs(n) == 1.0
+    even_sign = jnp.where(n == 0.0, 1.0, -1.0)
+    return jnp.where(odd, n * c, even_sign * s), jnp.where(odd, -n * s, even_sign * c)
 
 
 def kernel(
     nblk, ncol,
     pairing, offsets, weights, slab, angles,
     out, grad,
-    raw, land, angw, coef, sa, sb, field, adj, xa, xb, prod, stage, window,
+    raw, far, angw, coef, sa, sb, field, left_f, right_f, cut, adj, xa, xb, prod, stage, window,
     own_g, left_g, right_g, send_l, send_r,
-    load_sem, ang_sem, out_sem, h_send, h_recv, a_send, a_recv, o_send, o_recv, l_send, l_recv, r_send, r_recv,
+    load_sem, ang_sem, out_sem, n_send, n_recv, h_send, h_recv, a_send, a_recv,
+    o_send, o_recv, l_send, l_recv, r_send, r_recv,
 ):
     rows, width = slab.shape
     halves = width // LANES
@@ -72,18 +86,23 @@
         remote(angles.at[:, pl.ds(pairs - HALF, HALF)], angw.at[:, pl.ds(0, HALF)], a_send.at[0], a_recv.at[0], (after, col)),
         remote(angles.at[:, pl.ds(0, HALF)], angw.at[:, pl.ds(q_end, HALF)], a_send.at[1], a_recv.at[1], (before, col)),
     ]
-    halo_copies = []
+    near_copies = []
+    far_copies = []
     for h in range(halves):
         lanes = pl.ds(h * LANES, LANES)
-        halo_copies.append([
-            remote(slab.at[pl.ds(rows - SENT, SENT), lanes], land.at[h, 0], h_send.at[h, 0], h_recv.at[h, 0], (after, col)),
-            remote(slab.at[pl.ds(0, SENT), lanes], land.at[h, 1], h_send.at[h, 1], h_recv.at[h, 1], (before, col)),
+        near_copies += [
+            remote(slab.at[pl.ds(rows - 8, 8), lanes], raw.at[h, pl.ds(FRONT - 8, 8)], n_send.at[h, 0], n_recv.at[h, 0], (after, col)),
+            remote(slab.at[pl.ds(0, 8), lanes], raw.at[h, pl.ds(FRONT + rows, 8)], n_send.at[h, 1], n_recv.at[h, 1], (before, col)),
+        ]
+        far_copies.append([
+            remote(slab.at[pl.ds(rows - SENT, HALF), lanes], far.at[h, 0], h_send.at[h, 0], h_recv.at[h, 0], (after, col)),
+            remote(slab.at[pl.ds(8, HALF), lanes], far.at[h, 1], h_send.at[h, 1], h_recv.at[h, 1], (before, col)),
         ])
 
     pl.semaphore_wait(barrier, len(peers))
-    for copy in ang_copies:
+    for copy in ang_copies + near_copies:
         copy.start()
-    for pair in halo_copies:
+    for pair in far_copies:
         for copy in pair:
             copy.start()
 
@@ -92,19 +111,20 @@
     def zeros(n):
         return jnp.zeros((n, LANES), jnp.float32)
 
+    left_f[...] = zeros(left_f.shape[0])
+    right_f[...] = zeros(right_f.shape[0])
+    cut[...] = zeros(cut.shape[0])
     for h in range(halves):
         raw[h, 0:8, :] = zeros(8)
         raw[h, FRONT + rows + SENT:FRONT + rows + SENT + 16, :] = zeros(16)
         adj[h, 2 * q_lo:REACH - HALF, :] = zeros(REACH - HALF - 2 * q_lo)
         top = REACH + rows + HALF
         adj[h, top:2 * q_hi + 8, :] = zeros(2 * q_hi + 8 - top)
-        field[h, 0:2 * q_lo + 8, :] = zeros(2 * q_lo + 8)
-        field[h, 2 * q_hi:, :] = zeros(field.shape[1] - 2 * q_hi)
+        field[h, 0:REACH, :] = zeros(REACH)
+        field[h, REACH + rows:, :] = zeros(field.shape[1] - REACH - rows)
         for l in range(LAYERS):
             sa[h, l, q_hi:q_hi + 8, :] = zeros(8)
             sb[h, l, q_lo - 8:q_lo, :] = zeros(8)
-            prod[h, l, 0:q_lo, :] = zeros(q_lo)
-            prod[h, l, q_hi:total_q, :] = zeros(total_q - q_hi)
         for l in range(LAYERS - 1):
             xb[h, l, q_lo - 8:q_lo, :] = zeros(8)
             xa[h, l, q_hi:q_hi + 8, :] = zeros(8)
@@ -113,7 +133,11 @@
     for copy in ang_copies:
         copy.wait()
     theta = angw[...]
-    both = jnp.concatenate([jnp.cos(theta), jnp.sin(theta)], 0)
+    mid = total_q // 2
+    sine, cosine = sin_cos(jnp.concatenate([theta[:, :mid], theta[:, mid:]], 0))
+    both = jnp.concatenate([
+        jnp.concatenate([cosine[:LAYERS], sine[:LAYERS]], 0),
+        jnp.concatenate([cosine[LAYERS:], sine[LAYERS:]], 0)], 1)
     rolled = pltpu.roll(both, total_q - 1, 1)
     odd = lax.broadcasted_iota(jnp.int32, both.shape, 0) % 2 == 1
     moved = jnp.full(both.shape, first, jnp.int32) == 1
@@ -127,7 +151,14 @@
 
     sweep(0, total_q, LANES, spread)
 
-    def forward(h, low, high, step):
+    def held(h, l, q, n):
+        if l == LAYERS - 1:
+            return adj[h, pl.ds(2 * q + 1, n, stride=2), :], adj[h, pl.ds(2 * q + 2, n, stride=2), :]
+        if l % 2 == 1:
+            return xb[h, l, pl.ds(q, n), :], xa[h, l, pl.ds(q + 1, n), :]
+        return xb[h, l, pl.ds(q - 1, n), :], xa[h, l, pl.ds(q, n), :]
+
+    def forward(h, low, high, step, target, shift, products):
         for l in range(LAYERS):
             def body(q, l=l):
                 if l == 0:
@@ -145,63 +176,43 @@
                 new_b = s * a + c * b
                 sa[h, l, pl.ds(q, step), :] = new_a
                 sb[h, l, pl.ds(q, step), :] = new_b
+                if products:
+                    a, b = held(h, l, q, step)
+                    prod[h, l, pl.ds(q, step), :] = b * new_a - a * new_b
                 if l == LAYERS - 1:
-                    field[h, pl.ds(2 * q + 1, step, stride=2), :] = new_a
-                    field[h, pl.ds(2 * q + 2, step, stride=2), :] = new_b
+                    target[pl.ds(2 * q + 1 - shift, step, stride=2), :] = new_a
+                    target[pl.ds(2 * q + 2 - shift, step, stride=2), :] = new_b
             sweep(low, high, step, body)
-
-    def emit(h, low, high):
-        def body(r):
-            stage[h, pl.ds(r, 64), :] = field[h, pl.ds(r + REACH - first, 64), :]
-        sweep(low, high, 64, body)
-        return pltpu.make_async_copy(
-            stage.at[h, pl.ds(low, high - low)],
-            out.at[pl.ds(low, high - low), pl.ds(h * LANES, LANES)],
-            out_sem.at[h, 0 if low == 64 else (1 if low == 0 else 2)])
 
     reach = [offsets[k] for k in range(BANDS)]
     weight = [weights[k] for k in range(BANDS)]
 
-    def band(h, low, high, upper=True, lower=True, up_from=None, up_to=None, down_from=None, down_to=None):
+    def band(h, low, high, upper=None, lower=None, shift=0, more=False):
         n = 64
 
         def body(t):
-            acc = jnp.zeros((n, LANES), jnp.float32)
-            spot = lax.broadcasted_iota(jnp.int32, (n, LANES), 0)
+            acc = adj[h, pl.ds(t, n), :] if more else None
             for k in range(BANDS):
                 part = None
-                if upper:
-                    at = t + reach[k]
-                    part = field[h, pl.ds(at, n), :]
-                    if up_from is not None:
-                        part = jnp.where(spot >= up_from + REACH - at, part, 0.0)
-                    if up_to is not None:
-                        part = jnp.where(spot < up_to + REACH - at, part, 0.0)
-                if lower:
-                    at = t - reach[k]
-                    down = field[h, pl.ds(at, n), :]
-                    if down_from is not None:
-                        down = jnp.where(spot >= down_from + REACH - at, down, 0.0)
-                    if down_to is not None:
-                        down = jnp.where(spot < down_to + REACH - at, down, 0.0)
+                if upper is not None:
+                    part = upper[pl.ds(t - shift + reach[k], n), :]
+                if lower is not None:
+                    down = lower[pl.ds(t - shift - reach[k], n), :]
                     part = down if part is None else part + down
-                acc = acc + weight[k] * part
+                part = weight[k] * part
+                acc = part if acc is None else acc + part
             adj[h, pl.ds(t, n), :] = acc
         sweep(low + REACH, high + REACH, n, body)
 
-    def backward(h, low, high, step):
+    def backward(h, low, high, step, products):
         for l in reversed(range(LAYERS)):
+            if l == 0 and not products:
+                continue
+
             def body(q, l=l):
-                if l == LAYERS - 1:
-                    a = adj[h, pl.ds(2 * q + 1, step, stride=2), :]
-                    b = adj[h, pl.ds(2 * q + 2, step, stride=2), :]
-                elif l % 2 == 1:
-                    a = xb[h, l, pl.ds(q, step), :]
-                    b = xa[h, l, pl.ds(q + 1, step), :]
-                else:
-                    a = xb[h, l, pl.ds(q - 1, step), :]
-                    b = xa[h, l, pl.ds(q, step), :]
-                prod[h, l, pl.ds(q, step), :] = b * sa[h, l, pl.ds(q, step), :] - a * sb[h, l, pl.ds(q, step), :]
+                a, b = held(h, l, q, step)
+                if products:
+                    prod[h, l, pl.ds(q, step), :] = b * sa[h, l, pl.ds(q, step), :] - a * sb[h, l, pl.ds(q, step), :]
                 if l > 0:
                     c = coef[l, pl.ds(q, step), :]
                     s = coef[LAYERS + l, pl.ds(q, step), :]
@@ -209,47 +220,77 @@
                     xb[h, l - 1, pl.ds(q, step), :] = c * b - s * a
             sweep(low, high, step, body)
 
-    outs = []
+    def collapse(q, n, more):
+        start = q // LANES * LANES
+        wanted = (lax.broadcasted_iota(jnp.int32, (n, LANES), 0) + (q - start)
+                  == lax.broadcasted_iota(jnp.int32, (n, LANES), 1))
+        for l in range(LAYERS):
+            x = prod[0, l, q:q + n, :]
+            for h in range(1, halves):
+                x = x + prod[h, l, q:q + n, :]
+            s = jnp.sum(x, axis=1, keepdims=True)
+            line = jnp.sum(jnp.where(wanted, s, 0.0), axis=0, keepdims=True)
+            if more:
+                line = line + window[l:l + 1, start:start + LANES]
+            window[l:l + 1, start:start + LANES] = line
+
     for load in loads:
         load.wait()
-    for h in range(halves):
-        forward(h, q_own, q_end - 16, STEP)
-        outs.append(emit(h, 64, rows - 64))
+    for copy in near_copies:
+        copy.wait()
+    outs = []
+    edge = REACH + rows
+    for h in range(halves):
+        forward(h, q_own - 8, q_end + 8, 104, field.at[h], 0, False)
+
+        def emit(r, h=h):
+            stage[h, pl.ds(r, 128), :] = field[h, pl.ds(r + REACH - first, 128), :]
+
+        sweep(0, rows, 128, emit)
+        outs.append(pltpu.make_async_copy(stage.at[h], out.at[:, pl.ds(h * LANES, LANES)], out_sem.at[h]))
         outs[-1].start()
-        band(h, REACH + 16, rows - REACH - 48)
-        backward(h, q_own + 264, q_end - 280, STEP)
-
-    for h in range(halves):
-        for copy in halo_copies[h]:
+        field[h, REACH - 16:REACH, :] = zeros(16)
+        field[h, edge:edge + 24, :] = zeros(24)
+        cut[0:HALF, :] = field[h, rows:rows + HALF, :]
+        whole = field.at[h]
+        band(h, -HALF, 0, upper=whole)
+        band(h, 0, rows, upper=whole, lower=whole)
+        band(h, rows, rows + HALF, lower=cut, shift=rows)
+        backward(h, q_lo, q_own + 8, 144, False)
+        backward(h, q_own + 248, q_end - 248, 176, True)
+        backward(h, q_end - 136, q_hi, 136, True)
+    collapse(q_own + 264, 120, False)
+    for q in range(q_own + 384, q_end - 384, LANES):
+        collapse(q, LANES, False)
+    collapse(q_end - 384, 120, False)
+    collapse(q_end - 120, 120, False)
+
+    for h in range(halves):
+        for copy in far_copies[h]:
             copy.wait()
-        raw[h, 8:8 + SENT, :] = land[h, 0]
-        raw[h, FRONT + rows:FRONT + rows + SENT, :] = land[h, 1]
-        forward(h, q_lo, q_own + 8, STEP)
-        forward(h, q_end - 24, q_hi, 40)
-        for low, high in ((0, 64), (rows - 64, rows)):
-            outs.append(emit(h, low, high))
-            outs[-1].start()
-        band(h, -HALF, 0, lower=False, up_from=0)
-        band(h, 0, REACH + 64, down_from=-HALF)
-        band(h, rows - REACH - 64, rows - HALF)
-        band(h, rows - HALF, rows, up_to=rows)
-        band(h, rows, rows + HALF, upper=False, down_to=rows - HALF)
-        backward(h, q_lo, q_lo + 432, STEP)
-        backward(h, q_hi - 432, q_hi, STEP)
-
-    diagonal = (lax.broadcasted_iota(jnp.int32, (LANES, LANES), 0)
-                == lax.broadcasted_iota(jnp.int32, (LANES, LANES), 1))
-
-    def collapse(q):
-        for l in range(LAYERS):
-            x = prod[0, l, pl.ds(q, LANES), :]
-            for h in range(1, halves):
-                x = x + prod[h, l, pl.ds(q, LANES), :]
-            s = jnp.sum(x, axis=1, keepdims=True)
-            line = jnp.sum(jnp.where(diagonal, s, 0.0), axis=0, keepdims=True)
-            window[l:l + 1, pl.ds(pl.multiple_of(q, LANES), LANES)] = line
-
-    sweep(0, total_q, LANES, collapse)
+        raw[h, 8:8 + HALF, :] = far[h, 0]
+        raw[h, FRONT + rows + 8:FRONT + rows + SENT, :] = far[h, 1]
+        forward(h, q_lo, q_own, 136, left_f, 0, True)
+        forward(h, q_end - 8, q_hi, 144, right_f, rows, True)
+        left_f[2 * q_lo:HALF, :] = zeros(HALF - 2 * q_lo)
+        left_f[REACH:REACH + 8, :] = zeros(8)
+        right_f[REACH - 16:REACH, :] = zeros(16)
+        right_f[REACH + HALF:REACH + HALF + 24, :] = zeros(24)
+        band(h, 0, REACH, lower=left_f, more=True)
+        band(h, rows - REACH, rows - HALF, upper=right_f, shift=rows, more=True)
+        backward(h, q_own - 8, q_own + 264, 136, True)
+        backward(h, q_end - 264, q_end - 120, 144, True)
+    collapse(q_lo, 8, False)
+    collapse(LANES, LANES, False)
+    collapse(q_own, LANES, False)
+    collapse(q_own + LANES, LANES, False)
+    collapse(q_own + HALF, 8, True)
+    collapse(q_end - 264, 8, True)
+    collapse(q_end - HALF, LANES, False)
+    collapse(q_end - LANES, 8, True)
+    collapse(q_end, LANES, False)
+    collapse(q_end + LANES, 8, False)
+
     whole = window[...]
     rolled = pltpu.roll(whole, 1, 1)
     whole = jnp.where(jnp.logical_and(odd, moved), rolled, whole)[:LAYERS]
@@ -312,12 +353,15 @@
         out_specs=(anywhere, pl.BlockSpec(memory_space=pltpu.VMEM)),
         scratch_shapes=[
             pltpu.VMEM((halves, FRONT + rows + SENT + 16, LANES), f32),
-            pltpu.VMEM((halves, 2, SENT, LANES), f32),
+            pltpu.VMEM((halves, 2, HALF, LANES), f32),
             pltpu.VMEM((LAYERS, total_q), f32),
             pltpu.VMEM((2 * LAYERS, total_q, LANES), f32),
             pltpu.VMEM((halves, LAYERS, buf_q, LANES), f32),
             pltpu.VMEM((halves, LAYERS, buf_q, LANES), f32),
             pltpu.VMEM((halves, rows + 2 * REACH + 16, LANES), f32),
+            pltpu.VMEM((2 * REACH + 8, LANES), f32),
+            pltpu.VMEM((REACH + HALF + 24, LANES), f32),
+            pltpu.VMEM((REACH + HALF, LANES), f32),
             pltpu.VMEM((halves, rows + 2 * REACH + 16, LANES), f32),
             pltpu.VMEM((halves, LAYERS - 1, buf_q, LANES), f32),
             pltpu.VMEM((halves, LAYERS - 1, buf_q, LANES), f32),
@@ -329,7 +373,8 @@
             pltpu.VMEM((ncol, 2 * LAYERS, LANES), f32),
             pltpu.VMEM((2 * LAYERS, LANES), f32),
             pltpu.VMEM((2 * LAYERS, LANES), f32),
-            dma((halves,)), dma, dma((halves, 3)),
+            dma((halves,)), dma, dma((halves,)),
+            dma((halves, 2)), dma((halves, 2)),
             dma((halves, 2)), dma((halves, 2)),
             dma((2,)), dma((2,)),
             dma((ncol - 1,)), dma((ncol,)),

time: 37.8 us -> 35.4 us (0.937)
  Pallas kernels: 33.3 us -> 30.9 us
    pallas_call x1, Pallas kernels: 33.3 us -> 30.9 us  [on_device(): pl.pallas_call(functools.partial(kernel, nblk, ncol), out_shape=(jax.Shap...]
where the time goes in v2:
time: 35.4 us; the launch traced here: 35.2 us
  Pallas kernels  30.9 us (87%)
  local copies, waits for them, and re-layouts  3.66 us (10%)
  between operations  0.65 us (2%)
    pallas_call x1, Pallas kernels, on_device(): pl.pallas_call(functools.partial(kernel, nblk, ncol), out_shape=(jax.Shap...  30.9 us
    unnamed x4, local copies, waits for them, and re-layouts  3.66 us

profile of v2, /device:TPU:0, one launch (start us, length us, event | category | flops | bytes accessed | tf_op | source)
XLA Modules:
  0.0 35.2 jit_solution(9557691373513633168)
XLA Ops:
  0.6 30.9 %shard_map.68 = (f32[2048,256]{1,0:T(8,128)}, f32[4,1024]{1,0:T(4,128)}) custom-call(s32[4]{0:T(128)} %pairing.1, s32[8]{0:T(128)} %offsets.1, f32[8]{0:T(128)} %weights.1, f32[2048,256]{1,0:T(8,128)} %slab.1, f32[4,1024]{1,0:T(4,128)} %angles.1), custom_call_target="tpu_custom_call" | custom-call | tf_op jit(solution)/shard_map/pallas_call | solution.py:346
  31.5 0.0 copy-start
  31.5 3.0 %copy.9 = f32[2048,256]{1,0:T(8,128)} copy(f32[2048,256]{1,0:T(8,128)} %get-tuple-element.4) | data formatting | bytes 4194304
  34.6 0.0 copy-done
  34.6 0.6 %copy.10 = f32[4,1024]{1,0:T(4,128)} copy(f32[4,1024]{1,0:T(4,128)S(1)} %copy-done) | data formatting | bytes 32768
Async XLA Ops:
  31.5 3.1 %copy-start = (f32[4,1024]{1,0:T(4,128)S(1)}, f32[4,1024]{1,0:T(4,128)}, u32[]{:S(2)}) copy-start(f32[4,1024]{1,0:T(4,128)} %get-tuple-element.5) | copy-start | bytes 49156

commit v3 on v2

--- a/solution.py
+++ b/solution.py
@@ -45,9 +45,9 @@
     nblk, ncol,
     pairing, offsets, weights, slab, angles,
     out, grad,
-    raw, far, angw, coef, sa, sb, field, left_f, right_f, cut, adj, xa, xb, prod, stage, window,
+    raw, far, angw, coef, sa, sb, field, left_f, right_f, cut, adj, xa, xb, prod, window,
     own_g, left_g, right_g, send_l, send_r,
-    load_sem, ang_sem, out_sem, n_send, n_recv, h_send, h_recv, a_send, a_recv,
+    load_sem, ang_sem, n_send, n_recv, h_send, h_recv, a_send, a_recv,
     o_send, o_recv, l_send, l_recv, r_send, r_recv,
 ):
     rows, width = slab.shape
@@ -238,17 +238,14 @@
         load.wait()
     for copy in near_copies:
         copy.wait()
-    outs = []
     edge = REACH + rows
     for h in range(halves):
         forward(h, q_own - 8, q_end + 8, 104, field.at[h], 0, False)
 
         def emit(r, h=h):
-            stage[h, pl.ds(r, 128), :] = field[h, pl.ds(r + REACH - first, 128), :]
+            out[pl.ds(r, 128), h * LANES:(h + 1) * LANES] = field[h, pl.ds(r + REACH - first, 128), :]
 
         sweep(0, rows, 128, emit)
-        outs.append(pltpu.make_async_copy(stage.at[h], out.at[:, pl.ds(h * LANES, LANES)], out_sem.at[h]))
-        outs[-1].start()
         field[h, REACH - 16:REACH, :] = zeros(16)
         field[h, edge:edge + 24, :] = zeros(24)
         cut[0:HALF, :] = field[h, rows:rows + HALF, :]
@@ -329,7 +326,16 @@
         line[:, pairs - LANES:] + right[LAYERS:],
     ], 1)
     grad[...] = line
-    for copy in outs:
+
+
+def hand_out(evolved, gradient, evolved_out, gradient_out, sems):
+    copies = [
+        pltpu.make_async_copy(evolved, evolved_out, sems.at[0]),
+        pltpu.make_async_copy(gradient, gradient_out, sems.at[1]),
+    ]
+    for copy in copies:
+        copy.start()
+    for copy in copies:
         copy.wait()
 
 
@@ -343,14 +349,14 @@
     dma = pltpu.SemaphoreType.DMA
     smem = pl.BlockSpec(memory_space=pltpu.SMEM)
     anywhere = pl.BlockSpec(memory_space=pl.ANY)
-    return pl.pallas_call(
+    evolved, gradient = pl.pallas_call(
         functools.partial(kernel, nblk, ncol),
         out_shape=(
-            jax.ShapeDtypeStruct((rows, width), f32),
-            jax.ShapeDtypeStruct((LAYERS, pairs), f32),
+            pltpu.VMEM((rows, width), f32),
+            pltpu.VMEM((LAYERS, pairs), f32),
         ),
         in_specs=[smem, smem, smem, anywhere, anywhere],
-        out_specs=(anywhere, pl.BlockSpec(memory_space=pltpu.VMEM)),
+        out_specs=(pl.BlockSpec(memory_space=pltpu.VMEM), pl.BlockSpec(memory_space=pltpu.VMEM)),
         scratch_shapes=[
             pltpu.VMEM((halves, FRONT + rows + SENT + 16, LANES), f32),
             pltpu.VMEM((halves, 2, HALF, LANES), f32),
@@ -366,14 +372,13 @@
             pltpu.VMEM((halves, LAYERS - 1, buf_q, LANES), f32),
             pltpu.VMEM((halves, LAYERS - 1, buf_q, LANES), f32),
             pltpu.VMEM((halves, LAYERS, total_q, LANES), f32),
-            pltpu.VMEM((halves, rows, LANES), f32),
             pltpu.VMEM((2 * LAYERS, total_q), f32),
             pltpu.VMEM((ncol, 2 * LAYERS, pairs // 2), f32),
             pltpu.VMEM((ncol, 2 * LAYERS, LANES), f32),
             pltpu.VMEM((ncol, 2 * LAYERS, LANES), f32),
             pltpu.VMEM((2 * LAYERS, LANES), f32),
             pltpu.VMEM((2 * LAYERS, LANES), f32),
-            dma((halves,)), dma, dma((halves,)),
+            dma((halves,)), dma,
             dma((halves, 2)), dma((halves, 2)),
             dma((halves, 2)), dma((halves, 2)),
             dma((2,)), dma((2,)),
@@ -384,6 +389,16 @@
         compiler_params=pltpu.CompilerParams(
             collective_id=0, has_side_effects=True, vmem_limit_bytes=58 * 2**20),
     )(pairing, band_offsets, band_weights, slab, angles)
+    return pl.pallas_call(
+        hand_out,
+        out_shape=(
+            jax.ShapeDtypeStruct((rows, width), f32),
+            jax.ShapeDtypeStruct((LAYERS, pairs), f32),
+        ),
+        in_specs=[pl.BlockSpec(memory_space=pltpu.VMEM)] * 2,
+        out_specs=(anywhere, anywhere),
+        scratch_shapes=[dma((2,))],
+    )(evolved, gradient)
 
 
 def solution(mesh):

time: 35.4 us -> 36 us (1.017)
  Pallas kernels: 30.9 us -> 33.2 us
  local copies, waits for them, and re-layouts: 3.66 us -> 1.93 us
    pallas_call x1 -> x2, Pallas kernels: 30.9 us -> 33.2 us  [the longest x1 30.3 us: on_device(): pl.pallas_call(functools.partial(kernel, nblk, ncol), out_shape=(pltpu.VM...]
    unnamed x4, local copies, waits for them, and re-layouts: 3.66 us -> 1.93 us
where the time goes in v3:
time: 36 us; the launch traced here: 35.8 us
  Pallas kernels  33.2 us (92%)
  local copies, waits for them, and re-layouts  1.93 us (5%)
  between operations  0.65 us (2%)
    pallas_call x1, Pallas kernels, on_device(): pl.pallas_call(functools.partial(kernel, nblk, ncol), out_shape=(pltpu.VM...  30.3 us
    pallas_call x1, Pallas kernels, on_device(): pl.pallas_call(hand_out, out_shape=(jax.ShapeDtypeStruct((rows, width), f...  2.93 us
    unnamed x4, local copies, waits for them, and re-layouts  1.93 us

profile of v3, /device:TPU:0, one launch (start us, length us, event | category | flops | bytes accessed | tf_op | source)
XLA Modules:
  0.0 35.8 jit_solution(3414374536323256535)
XLA Ops:
  0.6 30.3 %shard_map.68 = (f32[2048,256]{1,0:T(8,128)S(1)}, f32[4,1024]{1,0:T(4,128)S(1)}) custom-call(s32[4]{0:T(128)} %pairing.1, s32[8]{0:T(128)} %offsets.1, f32[8]{0:T(128)} %weights.1, f32[2048,256]{1,0:T(8,128)} %slab.1, f32[4,1024]{1,0:T(4,128)} %angles.1), custom_call_target="tpu_custom_call" | custom-call | tf_op jit(solution)/shard_map/pallas_call | solution.py:352
  30.9 0.0 copy-start
  30.9 1.3 %copy-done = f32[2048,256]{1,0:T(8,128)} copy-done((f32[2048,256]{1,0:T(8,128)}, f32[2048,256]{1,0:T(8,128)S(1)}, u32[]{:S(2)}) %copy-start) | copy-done | bytes 2097176
  32.3 0.0 copy-start.1
  32.3 0.6 %copy-done.1 = f32[4,1024]{1,0:T(4,128)} copy-done((f32[4,1024]{1,0:T(4,128)}, f32[4,1024]{1,0:T(4,128)S(1)}, u32[]{:S(2)}) %copy-start.1) | copy-done | bytes 16408
  32.9 2.9 %shard_map.69 = (f32[2048,256]{1,0:T(8,128)}, f32[4,1024]{1,0:T(4,128)}) custom-call(f32[2048,256]{1,0:T(8,128)} %copy-done, f32[4,1024]{1,0:T(4,128)} %copy-done.1), custom_call_target="tpu_custom_call" | custom-call | tf_op jit(solution)/shard_map/pallas_call | solution.py:392
Async XLA Ops:
  30.9 1.3 %copy-start = (f32[2048,256]{1,0:T(8,128)}, f32[2048,256]{1,0:T(8,128)S(1)}, u32[]{:S(2)}) copy-start(f32[2048,256]{1,0:T(8,128)S(1)} %get-tuple-element.4.evolved) | copy-start | bytes 6291460
  32.3 0.6 %copy-start.1 = (f32[4,1024]{1,0:T(4,128)}, f32[4,1024]{1,0:T(4,128)S(1)}, u32[]{:S(2)}) copy-start(f32[4,1024]{1,0:T(4,128)S(1)} %get-tuple-element.5.gradient) | copy-start | bytes 49156

commit v4 on v2

--- a/solution.py
+++ b/solution.py
@@ -45,9 +45,9 @@
     nblk, ncol,
     pairing, offsets, weights, slab, angles,
     out, grad,
-    raw, far, angw, coef, sa, sb, field, left_f, right_f, cut, adj, xa, xb, prod, stage, window,
+    raw, far, angw, coef, sa, sb, field, left_f, right_f, cut, adj, xa, xb, prod, window,
     own_g, left_g, right_g, send_l, send_r,
-    load_sem, ang_sem, out_sem, n_send, n_recv, h_send, h_recv, a_send, a_recv,
+    load_sem, ang_sem, n_send, n_recv, h_send, h_recv, a_send, a_recv,
     o_send, o_recv, l_send, l_recv, r_send, r_recv,
 ):
     rows, width = slab.shape
@@ -122,34 +122,42 @@
         adj[h, top:2 * q_hi + 8, :] = zeros(2 * q_hi + 8 - top)
         field[h, 0:REACH, :] = zeros(REACH)
         field[h, REACH + rows:, :] = zeros(field.shape[1] - REACH - rows)
-        for l in range(LAYERS):
+        for l in range(LAYERS - 1):
             sa[h, l, q_hi:q_hi + 8, :] = zeros(8)
             sb[h, l, q_lo - 8:q_lo, :] = zeros(8)
-        for l in range(LAYERS - 1):
             xb[h, l, q_lo - 8:q_lo, :] = zeros(8)
             xa[h, l, q_hi:q_hi + 8, :] = zeros(8)
 
+    def coefficients(theta):
+        mid = theta.shape[1] // 2
+        sine, cosine = sin_cos(jnp.concatenate([theta[:, :mid], theta[:, mid:]], 0))
+        return jnp.concatenate([
+            jnp.concatenate([cosine[:LAYERS], sine[:LAYERS]], 0),
+            jnp.concatenate([cosine[LAYERS:], sine[LAYERS:]], 0)], 1)
+
+    def aligned(both):
+        rolled = pltpu.roll(both, both.shape[1] - 1, 1)
+        odd = lax.broadcasted_iota(jnp.int32, both.shape, 0) % 2 == 1
+        moved = jnp.full(both.shape, first, jnp.int32) == 1
+        return jnp.where(jnp.logical_and(odd, moved), rolled, both)
+
+    def spread(q):
+        turned = window[:, q:q + LANES].T
+        for j in range(2 * LAYERS):
+            coef[j, q:q + LANES, :] = jnp.broadcast_to(turned[:, j:j + 1], (LANES, LANES))
+
     own_ang.wait()
+    own_both = coefficients(angw[:, q_own:q_end])
+    window[:, q_own:q_end] = aligned(own_both)
+    for q in range(q_own, q_end - LANES, LANES):
+        spread(q)
     for copy in ang_copies:
         copy.wait()
-    theta = angw[...]
-    mid = total_q // 2
-    sine, cosine = sin_cos(jnp.concatenate([theta[:, :mid], theta[:, mid:]], 0))
-    both = jnp.concatenate([
-        jnp.concatenate([cosine[:LAYERS], sine[:LAYERS]], 0),
-        jnp.concatenate([cosine[LAYERS:], sine[LAYERS:]], 0)], 1)
-    rolled = pltpu.roll(both, total_q - 1, 1)
-    odd = lax.broadcasted_iota(jnp.int32, both.shape, 0) % 2 == 1
-    moved = jnp.full(both.shape, first, jnp.int32) == 1
-    window[...] = jnp.where(jnp.logical_and(odd, moved), rolled, both)
-
-    def spread(q):
-        part = window[:, pl.ds(pl.multiple_of(q, LANES), LANES)]
-        turned = part.T
-        for j in range(2 * LAYERS):
-            coef[j, pl.ds(q, LANES), :] = jnp.broadcast_to(turned[:, j:j + 1], (LANES, LANES))
-
-    sweep(0, total_q, LANES, spread)
+    left_both = coefficients(angw[:, :q_own])
+    right_both = coefficients(angw[:, q_end:])
+    window[...] = aligned(jnp.concatenate([left_both, own_both, right_both], 1))
+    for q in (0, LANES, q_end - LANES, q_end, q_end + LANES):
+        spread(q)
 
     def held(h, l, q, n):
         if l == LAYERS - 1:
@@ -174,8 +182,9 @@
                 s = coef[LAYERS + l, pl.ds(q, step), :]
                 new_a = c * a - s * b
                 new_b = s * a + c * b
-                sa[h, l, pl.ds(q, step), :] = new_a
-                sb[h, l, pl.ds(q, step), :] = new_b
+                if l < LAYERS - 1:
+                    sa[h, l, pl.ds(q, step), :] = new_a
+                    sb[h, l, pl.ds(q, step), :] = new_b
                 if products:
                     a, b = held(h, l, q, step)
                     prod[h, l, pl.ds(q, step), :] = b * new_a - a * new_b
@@ -188,7 +197,7 @@
     weight = [weights[k] for k in range(BANDS)]
 
     def band(h, low, high, upper=None, lower=None, shift=0, more=False):
-        n = 64
+        n = 128
 
         def body(t):
             acc = adj[h, pl.ds(t, n), :] if more else None
@@ -211,13 +220,18 @@
 
             def body(q, l=l):
                 a, b = held(h, l, q, step)
-                if products:
-                    prod[h, l, pl.ds(q, step), :] = b * sa[h, l, pl.ds(q, step), :] - a * sb[h, l, pl.ds(q, step), :]
                 if l > 0:
                     c = coef[l, pl.ds(q, step), :]
                     s = coef[LAYERS + l, pl.ds(q, step), :]
-                    xa[h, l - 1, pl.ds(q, step), :] = c * a + s * b
-                    xb[h, l - 1, pl.ds(q, step), :] = c * b - s * a
+                    new_a = c * a + s * b
+                    new_b = c * b - s * a
+                    xa[h, l - 1, pl.ds(q, step), :] = new_a
+                    xb[h, l - 1, pl.ds(q, step), :] = new_b
+                if products and l % 2 == 0:
+                    prod[h, l, pl.ds(q, step), :] = b * sa[h, l, pl.ds(q, step), :] - a * sb[h, l, pl.ds(q, step), :]
+                elif products:
+                    prod[h, l, pl.ds(q, step), :] = (
+                        new_b * sb[h, l - 1, pl.ds(q, step), :] - new_a * sa[h, l - 1, pl.ds(q + 1, step), :])
             sweep(low, high, step, body)
 
     def collapse(q, n, more):
@@ -238,17 +252,14 @@
         load.wait()
     for copy in near_copies:
         copy.wait()
-    outs = []
     edge = REACH + rows
     for h in range(halves):
         forward(h, q_own - 8, q_end + 8, 104, field.at[h], 0, False)
 
         def emit(r, h=h):
-            stage[h, pl.ds(r, 128), :] = field[h, pl.ds(r + REACH - first, 128), :]
+            out[pl.ds(r, 128), h * LANES:(h + 1) * LANES] = field[h, pl.ds(r + REACH - first, 128), :]
 
         sweep(0, rows, 128, emit)
-        outs.append(pltpu.make_async_copy(stage.at[h], out.at[:, pl.ds(h * LANES, LANES)], out_sem.at[h]))
-        outs[-1].start()
         field[h, REACH - 16:REACH, :] = zeros(16)
         field[h, edge:edge + 24, :] = zeros(24)
         cut[0:HALF, :] = field[h, rows:rows + HALF, :]
@@ -293,6 +304,8 @@
 
     whole = window[...]
     rolled = pltpu.roll(whole, 1, 1)
+    odd = lax.broadcasted_iota(jnp.int32, whole.shape, 0) % 2 == 1
+    moved = jnp.full(whole.shape, first, jnp.int32) == 1
     whole = jnp.where(jnp.logical_and(odd, moved), rolled, whole)[:LAYERS]
     mid = q_own + pairs // 2
     own_g[pl.ds(col, 1)] = jnp.concatenate([whole[:, q_own:mid], whole[:, mid:q_end]], 0)[None]
@@ -329,8 +342,6 @@
         line[:, pairs - LANES:] + right[LAYERS:],
     ], 1)
     grad[...] = line
-    for copy in outs:
-        copy.wait()
 
 
 def on_device(nblk, ncol, slab, angles, pairing, band_offsets, band_weights):
@@ -346,18 +357,18 @@
     return pl.pallas_call(
         functools.partial(kernel, nblk, ncol),
         out_shape=(
-            jax.ShapeDtypeStruct((rows, width), f32),
-            jax.ShapeDtypeStruct((LAYERS, pairs), f32),
+            pltpu.VMEM((rows, width), f32),
+            pltpu.VMEM((LAYERS, pairs), f32),
         ),
         in_specs=[smem, smem, smem, anywhere, anywhere],
-        out_specs=(anywhere, pl.BlockSpec(memory_space=pltpu.VMEM)),
+        out_specs=(pl.BlockSpec(memory_space=pltpu.VMEM), pl.BlockSpec(memory_space=pltpu.VMEM)),
         scratch_shapes=[
             pltpu.VMEM((halves, FRONT + rows + SENT + 16, LANES), f32),
             pltpu.VMEM((halves, 2, HALF, LANES), f32),
             pltpu.VMEM((LAYERS, total_q), f32),
             pltpu.VMEM((2 * LAYERS, total_q, LANES), f32),
-            pltpu.VMEM((halves, LAYERS, buf_q, LANES), f32),
-            pltpu.VMEM((halves, LAYERS, buf_q, LANES), f32),
+            pltpu.VMEM((halves, LAYERS - 1, buf_q, LANES), f32),
+            pltpu.VMEM((halves, LAYERS - 1, buf_q, LANES), f32),
             pltpu.VMEM((halves, rows + 2 * REACH + 16, LANES), f32),
             pltpu.VMEM((2 * REACH + 8, LANES), f32),
             pltpu.VMEM((REACH + HALF + 24, LANES), f32),
@@ -366,14 +377,13 @@
             pltpu.VMEM((halves, LAYERS - 1, buf_q, LANES), f32),
             pltpu.VMEM((halves, LAYERS - 1, buf_q, LANES), f32),
             pltpu.VMEM((halves, LAYERS, total_q, LANES), f32),
-            pltpu.VMEM((halves, rows, LANES), f32),
             pltpu.VMEM((2 * LAYERS, total_q), f32),
             pltpu.VMEM((ncol, 2 * LAYERS, pairs // 2), f32),
             pltpu.VMEM((ncol, 2 * LAYERS, LANES), f32),
             pltpu.VMEM((ncol, 2 * LAYERS, LANES), f32),
             pltpu.VMEM((2 * LAYERS, LANES), f32),
             pltpu.VMEM((2 * LAYERS, LANES), f32),
-            dma((halves,)), dma, dma((halves,)),
+            dma((halves,)), dma,
             dma((halves, 2)), dma((halves, 2)),
             dma((halves, 2)), dma((halves, 2)),
             dma((2,)), dma((2,)),

time: 35.4 us -> 30.2 us (0.85)
  Pallas kernels: 30.9 us -> 27.4 us
  local copies, waits for them, and re-layouts: 3.66 us -> 1.93 us
    pallas_call x1, Pallas kernels: 30.9 us -> 27.4 us  [on_device(): pl.pallas_call(functools.partial(kernel, nblk, ncol), out_shape=(pltpu.VM...]
    unnamed x4 -> x2, local copies, waits for them, and re-layouts: 3.66 us -> 1.93 us
where the time goes in v4:
time: 30.2 us; the launch traced here: 30 us
  Pallas kernels  27.4 us (91%)
  local copies, waits for them, and re-layouts  1.93 us (6%)
  between operations  0.64 us (2%)
    pallas_call x1, Pallas kernels, on_device(): pl.pallas_call(functools.partial(kernel, nblk, ncol), out_shape=(pltpu.VM...  27.4 us
    unnamed x2, local copies, waits for them, and re-layouts  1.93 us

profile of v4, /device:TPU:0, one launch (start us, length us, event | category | flops | bytes accessed | tf_op | source)
XLA Modules:
  0.0 30.0 jit_solution(17565204066278139172)
XLA Ops:
  0.6 27.4 %shard_map.68 = (f32[2048,256]{1,0:T(8,128)S(1)}, f32[4,1024]{1,0:T(4,128)S(1)}) custom-call(s32[4]{0:T(128)} %pairing.1, s32[8]{0:T(128)} %offsets.1, f32[8]{0:T(128)} %weights.1, f32[2048,256]{1,0:T(8,128)} %slab.1, f32[4,1024]{1,0:T(4,128)} %angles.1), custom_call_target="tpu_custom_call" | custom-call | tf_op jit(solution)/shard_map/pallas_call | solution.py:357
  28.0 1.3 %copy.9 = f32[2048,256]{1,0:T(8,128)} copy(f32[2048,256]{1,0:T(8,128)S(1)} %get-tuple-element.2) | data formatting | bytes 4194304
  29.4 0.6 %copy.10 = f32[4,1024]{1,0:T(4,128)} copy(f32[4,1024]{1,0:T(4,128)S(1)} %get-tuple-element.3) | data formatting | bytes 32768

commit v5 on v4

--- a/solution.py
+++ b/solution.py
@@ -99,13 +99,6 @@
             remote(slab.at[pl.ds(8, HALF), lanes], far.at[h, 1], h_send.at[h, 1], h_recv.at[h, 1], (before, col)),
         ])
 
-    pl.semaphore_wait(barrier, len(peers))
-    for copy in ang_copies + near_copies:
-        copy.start()
-    for pair in far_copies:
-        for copy in pair:
-            copy.start()
-
     first = pairing[0]
 
     def zeros(n):
@@ -141,23 +134,33 @@
         moved = jnp.full(both.shape, first, jnp.int32) == 1
         return jnp.where(jnp.logical_and(odd, moved), rolled, both)
 
-    def spread(q):
-        turned = window[:, q:q + LANES].T
+    def spread(q, low=0, n=LANES):
+        turned = window[:, q:q + LANES].T[low:low + n]
         for j in range(2 * LAYERS):
-            coef[j, q:q + LANES, :] = jnp.broadcast_to(turned[:, j:j + 1], (LANES, LANES))
+            coef[j, q + low:q + low + n, :] = jnp.broadcast_to(turned[:, j:j + 1], (n, LANES))
 
     own_ang.wait()
     own_both = coefficients(angw[:, q_own:q_end])
     window[:, q_own:q_end] = aligned(own_both)
     for q in range(q_own, q_end - LANES, LANES):
         spread(q)
+
+    pl.semaphore_wait(barrier, len(peers))
+    for copy in ang_copies + near_copies:
+        copy.start()
+    for pair in far_copies:
+        for copy in pair:
+            copy.start()
+
     for copy in ang_copies:
         copy.wait()
     left_both = coefficients(angw[:, :q_own])
     right_both = coefficients(angw[:, q_end:])
     window[...] = aligned(jnp.concatenate([left_both, own_both, right_both], 1))
-    for q in (0, LANES, q_end - LANES, q_end, q_end + LANES):
+    spread(0, q_lo, 8)
+    for q in (LANES, q_end - LANES, q_end):
         spread(q)
+    spread(q_end + LANES, 0, 8)
 
     def held(h, l, q, n):
         if l == LAYERS - 1:
@@ -166,31 +169,33 @@
             return xb[h, l, pl.ds(q, n), :], xa[h, l, pl.ds(q + 1, n), :]
         return xb[h, l, pl.ds(q - 1, n), :], xa[h, l, pl.ds(q, n), :]
 
-    def forward(h, low, high, step, target, shift, products):
+    def forward(halves_in, low, high, step, target, shift, products):
         for l in range(LAYERS):
             def body(q, l=l):
-                if l == 0:
-                    a = raw[h, pl.ds(2 * q - 2 * q_lo + first, step, stride=2), :]
-                    b = raw[h, pl.ds(2 * q - 2 * q_lo + 1 + first, step, stride=2), :]
-                elif l % 2 == 1:
-                    a = sb[h, l - 1, pl.ds(q, step), :]
-                    b = sa[h, l - 1, pl.ds(q + 1, step), :]
-                else:
-                    a = sb[h, l - 1, pl.ds(q - 1, step), :]
-                    b = sa[h, l - 1, pl.ds(q, step), :]
                 c = coef[l, pl.ds(q, step), :]
                 s = coef[LAYERS + l, pl.ds(q, step), :]
-                new_a = c * a - s * b
-                new_b = s * a + c * b
-                if l < LAYERS - 1:
-                    sa[h, l, pl.ds(q, step), :] = new_a
-                    sb[h, l, pl.ds(q, step), :] = new_b
-                if products:
-                    a, b = held(h, l, q, step)
-                    prod[h, l, pl.ds(q, step), :] = b * new_a - a * new_b
-                if l == LAYERS - 1:
-                    target[pl.ds(2 * q + 1 - shift, step, stride=2), :] = new_a
-                    target[pl.ds(2 * q + 2 - shift, step, stride=2), :] = new_b
+                for h in halves_in:
+                    if l == 0:
+                        a = raw[h, pl.ds(2 * q - 2 * q_lo + first, step, stride=2), :]
+                        b = raw[h, pl.ds(2 * q - 2 * q_lo + 1 + first, step, stride=2), :]
+                    elif l % 2 == 1:
+                        a = sb[h, l - 1, pl.ds(q, step), :]
+                        b = sa[h, l - 1, pl.ds(q + 1, step), :]
+                    else:
+                        a = sb[h, l - 1, pl.ds(q - 1, step), :]
+                        b = sa[h, l - 1, pl.ds(q, step), :]
+                    new_a = c * a - s * b
+                    new_b = s * a + c * b
+                    if l < LAYERS - 1:
+                        sa[h, l, pl.ds(q, step), :] = new_a
+                        sb[h, l, pl.ds(q, step), :] = new_b
+                    if products:
+                        a, b = held(h, l, q, step)
+                        prod[h, l, pl.ds(q, step), :] = b * new_a - a * new_b
+                    if l == LAYERS - 1:
+                        into = target(h)
+                        into[pl.ds(2 * q + 1 - shift, step, stride=2), :] = new_a
+                        into[pl.ds(2 * q + 2 - shift, step, stride=2), :] = new_b
             sweep(low, high, step, body)
 
     reach = [offsets[k] for k in range(BANDS)]
@@ -213,25 +218,27 @@
             adj[h, pl.ds(t, n), :] = acc
         sweep(low + REACH, high + REACH, n, body)
 
-    def backward(h, low, high, step, products):
+    def backward(halves_in, low, high, step, products):
         for l in reversed(range(LAYERS)):
             if l == 0 and not products:
                 continue
 
             def body(q, l=l):
-                a, b = held(h, l, q, step)
                 if l > 0:
                     c = coef[l, pl.ds(q, step), :]
                     s = coef[LAYERS + l, pl.ds(q, step), :]
-                    new_a = c * a + s * b
-                    new_b = c * b - s * a
-                    xa[h, l - 1, pl.ds(q, step), :] = new_a
-                    xb[h, l - 1, pl.ds(q, step), :] = new_b
-                if products and l % 2 == 0:
-                    prod[h, l, pl.ds(q, step), :] = b * sa[h, l, pl.ds(q, step), :] - a * sb[h, l, pl.ds(q, step), :]
-                elif products:
-                    prod[h, l, pl.ds(q, step), :] = (
-                        new_b * sb[h, l - 1, pl.ds(q, step), :] - new_a * sa[h, l - 1, pl.ds(q + 1, step), :])
+                for h in halves_in:
+                    a, b = held(h, l, q, step)
+                    if l > 0:
+                        new_a = c * a + s * b
+                        new_b = c * b - s * a
+                        xa[h, l - 1, pl.ds(q, step), :] = new_a
+                        xb[h, l - 1, pl.ds(q, step), :] = new_b
+                    if products and l % 2 == 0:
+                        prod[h, l, pl.ds(q, step), :] = b * sa[h, l, pl.ds(q, step), :] - a * sb[h, l, pl.ds(q, step), :]
+                    elif products:
+                        prod[h, l, pl.ds(q, step), :] = (
+                            new_b * sb[h, l - 1, pl.ds(q, step), :] - new_a * sa[h, l - 1, pl.ds(q + 1, step), :])
             sweep(low, high, step, body)
 
     def collapse(q, n, more):
@@ -253,13 +260,15 @@
     for copy in near_copies:
         copy.wait()
     edge = REACH + rows
-    for h in range(halves):
-        forward(h, q_own - 8, q_end + 8, 104, field.at[h], 0, False)
-
-        def emit(r, h=h):
+    both_halves = range(halves)
+    forward(both_halves, q_own - 8, q_end + 8, 104, lambda h: field.at[h], 0, False)
+
+    def emit(r):
+        for h in both_halves:
             out[pl.ds(r, 128), h * LANES:(h + 1) * LANES] = field[h, pl.ds(r + REACH - first, 128), :]
 
-        sweep(0, rows, 128, emit)
+    sweep(0, rows, 128, emit)
+    for h in both_halves:
         field[h, REACH - 16:REACH, :] = zeros(16)
         field[h, edge:edge + 24, :] = zeros(24)
         cut[0:HALF, :] = field[h, rows:rows + HALF, :]
@@ -267,9 +276,9 @@
         band(h, -HALF, 0, upper=whole)
         band(h, 0, rows, upper=whole, lower=whole)
         band(h, rows, rows + HALF, lower=cut, shift=rows)
-        backward(h, q_lo, q_own + 8, 144, False)
-        backward(h, q_own + 248, q_end - 248, 176, True)
-        backward(h, q_end - 136, q_hi, 136, True)
+    backward(both_halves, q_lo, q_own + 8, 72, False)
+    backward(both_halves, q_own + 248, q_end - 248, 88, True)
+    backward(both_halves, q_end - 136, q_hi, 136, True)
     collapse(q_own + 264, 120, False)
     for q in range(q_own + 384, q_end - 384, LANES):
         collapse(q, LANES, False)
@@ -281,16 +290,16 @@
             copy.wait()
         raw[h, 8:8 + HALF, :] = far[h, 0]
         raw[h, FRONT + rows + 8:FRONT + rows + SENT, :] = far[h, 1]
-        forward(h, q_lo, q_own, 136, left_f, 0, True)
-        forward(h, q_end - 8, q_hi, 144, right_f, rows, True)
+        forward([h], q_lo, q_own, 136, lambda h: left_f, 0, True)
+        forward([h], q_end - 8, q_hi, 144, lambda h: right_f, rows, True)
         left_f[2 * q_lo:HALF, :] = zeros(HALF - 2 * q_lo)
         left_f[REACH:REACH + 8, :] = zeros(8)
         right_f[REACH - 16:REACH, :] = zeros(16)
         right_f[REACH + HALF:REACH + HALF + 24, :] = zeros(24)
         band(h, 0, REACH, lower=left_f, more=True)
         band(h, rows - REACH, rows - HALF, upper=right_f, shift=rows, more=True)
-        backward(h, q_own - 8, q_own + 264, 136, True)
-        backward(h, q_end - 264, q_end - 120, 144, True)
+        backward([h], q_own - 8, q_own + 264, 136, True)
+        backward([h], q_end - 264, q_end - 120, 144, True)
     collapse(q_lo, 8, False)
     collapse(LANES, LANES, False)
     collapse(q_own, LANES, False)

time: 30.2 us -> 30.4 us (level)
    pallas_call x1, Pallas kernels: 27.4 us -> 27.7 us  [on_device(): pl.pallas_call(functools.partial(kernel, nblk, ncol), out_shape=(pltpu.VM...]
where the time goes in v5:
time: 30.4 us; the launch traced here: 30.3 us
  Pallas kernels  27.7 us (91%)
  local copies, waits for them, and re-layouts  1.93 us (6%)
  between operations  0.64 us (2%)
    pallas_call x1, Pallas kernels, on_device(): pl.pallas_call(functools.partial(kernel, nblk, ncol), out_shape=(pltpu.VM...  27.7 us
    unnamed x2, local copies, waits for them, and re-layouts  1.93 us

profile of v5, /device:TPU:0, one launch (start us, length us, event | category | flops | bytes accessed | tf_op | source)
XLA Modules:
  0.0 30.3 jit_solution(631339818331650359)
XLA Ops:
  0.6 27.7 %shard_map.68 = (f32[2048,256]{1,0:T(8,128)S(1)}, f32[4,1024]{1,0:T(4,128)S(1)}) custom-call(s32[4]{0:T(128)} %pairing.1, s32[8]{0:T(128)} %offsets.1, f32[8]{0:T(128)} %weights.1, f32[2048,256]{1,0:T(8,128)} %slab.1, f32[4,1024]{1,0:T(4,128)} %angles.1), custom_call_target="tpu_custom_call" | custom-call | tf_op jit(solution)/shard_map/pallas_call | solution.py:366
  28.4 1.3 %copy.9 = f32[2048,256]{1,0:T(8,128)} copy(f32[2048,256]{1,0:T(8,128)S(1)} %get-tuple-element.2) | data formatting | bytes 4194304
  29.7 0.6 %copy.10 = f32[4,1024]{1,0:T(4,128)} copy(f32[4,1024]{1,0:T(4,128)S(1)} %get-tuple-element.3) | data formatting | bytes 32768

commit v6 on v5

--- a/solution.py
+++ b/solution.py
@@ -101,6 +101,34 @@
 
     first = pairing[0]
 
+    def coefficients(theta):
+        mid = theta.shape[1] // 2
+        sine, cosine = sin_cos(jnp.concatenate([theta[:, :mid], theta[:, mid:]], 0))
+        return jnp.concatenate([
+            jnp.concatenate([cosine[:LAYERS], sine[:LAYERS]], 0),
+            jnp.concatenate([cosine[LAYERS:], sine[LAYERS:]], 0)], 1)
+
+    def aligned(both):
+        rolled = pltpu.roll(both, both.shape[1] - 1, 1)
+        odd = lax.broadcasted_iota(jnp.int32, both.shape, 0) % 2 == 1
+        moved = jnp.full(both.shape, first, jnp.int32) == 1
+        return jnp.where(jnp.logical_and(odd, moved), rolled, both)
+
+    def spread(q, low=0, n=LANES):
+        turned = window[:, q:q + LANES].T[low:low + n]
+        for j in range(2 * LAYERS):
+            coef[j, q + low:q + low + n, :] = jnp.broadcast_to(turned[:, j:j + 1], (n, LANES))
+
+    own_ang.wait()
+    own_both = coefficients(angw[:, q_own:q_end])
+    window[:, q_own:q_end] = aligned(own_both)
+    for q in range(q_own, q_end - LANES, LANES):
+        spread(q)
+
+    pl.semaphore_wait(barrier, len(peers))
+    for copy in ang_copies + near_copies + far_copies[0]:
+        copy.start()
+
     def zeros(n):
         return jnp.zeros((n, LANES), jnp.float32)
 
@@ -120,37 +148,6 @@
             sb[h, l, q_lo - 8:q_lo, :] = zeros(8)
             xb[h, l, q_lo - 8:q_lo, :] = zeros(8)
             xa[h, l, q_hi:q_hi + 8, :] = zeros(8)
-
-    def coefficients(theta):
-        mid = theta.shape[1] // 2
-        sine, cosine = sin_cos(jnp.concatenate([theta[:, :mid], theta[:, mid:]], 0))
-        return jnp.concatenate([
-            jnp.concatenate([cosine[:LAYERS], sine[:LAYERS]], 0),
-            jnp.concatenate([cosine[LAYERS:], sine[LAYERS:]], 0)], 1)
-
-    def aligned(both):
-        rolled = pltpu.roll(both, both.shape[1] - 1, 1)
-        odd = lax.broadcasted_iota(jnp.int32, both.shape, 0) % 2 == 1
-        moved = jnp.full(both.shape, first, jnp.int32) == 1
-        return jnp.where(jnp.logical_and(odd, moved), rolled, both)
-
-    def spread(q, low=0, n=LANES):
-        turned = window[:, q:q + LANES].T[low:low + n]
-        for j in range(2 * LAYERS):
-            coef[j, q + low:q + low + n, :] = jnp.broadcast_to(turned[:, j:j + 1], (n, LANES))
-
-    own_ang.wait()
-    own_both = coefficients(angw[:, q_own:q_end])
-    window[:, q_own:q_end] = aligned(own_both)
-    for q in range(q_own, q_end - LANES, LANES):
-        spread(q)
-
-    pl.semaphore_wait(barrier, len(peers))
-    for copy in ang_copies + near_copies:
-        copy.start()
-    for pair in far_copies:
-        for copy in pair:
-            copy.start()
 
     for copy in ang_copies:
         copy.wait()
@@ -255,20 +252,22 @@
                 line = line + window[l:l + 1, start:start + LANES]
             window[l:l + 1, start:start + LANES] = line
 
+    for pair in far_copies[1:]:
+        for copy in pair:
+            copy.start()
+
     for load in loads:
         load.wait()
     for copy in near_copies:
         copy.wait()
     edge = REACH + rows
-    both_halves = range(halves)
-    forward(both_halves, q_own - 8, q_end + 8, 104, lambda h: field.at[h], 0, False)
-
-    def emit(r):
-        for h in both_halves:
+    for h in range(halves):
+        forward([h], q_own - 8, q_end + 8, 104, lambda h: field.at[h], 0, False)
+
+        def emit(r, h=h):
             out[pl.ds(r, 128), h * LANES:(h + 1) * LANES] = field[h, pl.ds(r + REACH - first, 128), :]
 
-    sweep(0, rows, 128, emit)
-    for h in both_halves:
+        sweep(0, rows, 128, emit)
         field[h, REACH - 16:REACH, :] = zeros(16)
         field[h, edge:edge + 24, :] = zeros(24)
         cut[0:HALF, :] = field[h, rows:rows + HALF, :]
@@ -276,9 +275,9 @@
         band(h, -HALF, 0, upper=whole)
         band(h, 0, rows, upper=whole, lower=whole)
         band(h, rows, rows + HALF, lower=cut, shift=rows)
-    backward(both_halves, q_lo, q_own + 8, 72, False)
-    backward(both_halves, q_own + 248, q_end - 248, 88, True)
-    backward(both_halves, q_end - 136, q_hi, 136, True)
+        backward([h], q_lo, q_own + 8, 144, False)
+        backward([h], q_own + 248, q_end - 248, 176, True)
+        backward([h], q_end - 136, q_hi, 136, True)
     collapse(q_own + 264, 120, False)
     for q in range(q_own + 384, q_end - 384, LANES):
         collapse(q, LANES, False)

time: 30.4 us -> 29.7 us (0.977)
  Pallas kernels: 27.7 us -> 26.9 us
    pallas_call x1, Pallas kernels: 27.7 us -> 26.9 us  [on_device(): pl.pallas_call(functools.partial(kernel, nblk, ncol), out_shape=(pltpu.VM...]
where the time goes in v6:
time: 29.7 us; the launch traced here: 29.5 us
  Pallas kernels  26.9 us (91%)
  local copies, waits for them, and re-layouts  1.93 us (6%)
  between operations  0.64 us (2%)
    pallas_call x1, Pallas kernels, on_device(): pl.pallas_call(functools.partial(kernel, nblk, ncol), out_shape=(pltpu.VM...  26.9 us
    unnamed x2, local copies, waits for them, and re-layouts  1.93 us

profile of v6, /device:TPU:0, one launch (start us, length us, event | category | flops | bytes accessed | tf_op | source)
XLA Modules:
  0.0 29.5 jit_solution(5508551575002592582)
XLA Ops:
  0.6 26.9 %shard_map.68 = (f32[2048,256]{1,0:T(8,128)S(1)}, f32[4,1024]{1,0:T(4,128)S(1)}) custom-call(s32[4]{0:T(128)} %pairing.1, s32[8]{0:T(128)} %offsets.1, f32[8]{0:T(128)} %weights.1, f32[2048,256]{1,0:T(8,128)} %slab.1, f32[4,1024]{1,0:T(4,128)} %angles.1), custom_call_target="tpu_custom_call" | custom-call | tf_op jit(solution)/shard_map/pallas_call | solution.py:365
  27.6 1.3 %copy.9 = f32[2048,256]{1,0:T(8,128)} copy(f32[2048,256]{1,0:T(8,128)S(1)} %get-tuple-element.2) | data formatting | bytes 4194304
  28.9 0.6 %copy.10 = f32[4,1024]{1,0:T(4,128)} copy(f32[4,1024]{1,0:T(4,128)S(1)} %get-tuple-element.3) | data formatting | bytes 32768

commit v7 on v5

--- a/solution.py
+++ b/solution.py
@@ -45,7 +45,7 @@
     nblk, ncol,
     pairing, offsets, weights, slab, angles,
     out, grad,
-    raw, far, angw, coef, sa, sb, field, left_f, right_f, cut, adj, xa, xb, prod, window,
+    raw, near, far, angw, coef, sa, sb, field, left_f, right_f, cut, adj, xa, xb, prod, window,
     own_g, left_g, right_g, send_l, send_r,
     load_sem, ang_sem, n_send, n_recv, h_send, h_recv, a_send, a_recv,
     o_send, o_recv, l_send, l_recv, r_send, r_recv,
@@ -91,8 +91,8 @@
     for h in range(halves):
         lanes = pl.ds(h * LANES, LANES)
         near_copies += [
-            remote(slab.at[pl.ds(rows - 8, 8), lanes], raw.at[h, pl.ds(FRONT - 8, 8)], n_send.at[h, 0], n_recv.at[h, 0], (after, col)),
-            remote(slab.at[pl.ds(0, 8), lanes], raw.at[h, pl.ds(FRONT + rows, 8)], n_send.at[h, 1], n_recv.at[h, 1], (before, col)),
+            remote(slab.at[pl.ds(rows - 8, 8), lanes], near.at[h, 0], n_send.at[h, 0], n_recv.at[h, 0], (after, col)),
+            remote(slab.at[pl.ds(0, 8), lanes], near.at[h, 1], n_send.at[h, 1], n_recv.at[h, 1], (before, col)),
         ]
         far_copies.append([
             remote(slab.at[pl.ds(rows - SENT, HALF), lanes], far.at[h, 0], h_send.at[h, 0], h_recv.at[h, 0], (after, col)),
@@ -146,21 +146,8 @@
         spread(q)
 
     pl.semaphore_wait(barrier, len(peers))
-    for copy in ang_copies + near_copies:
+    for copy in ang_copies + near_copies + far_copies[0]:
         copy.start()
-    for pair in far_copies:
-        for copy in pair:
-            copy.start()
-
-    for copy in ang_copies:
-        copy.wait()
-    left_both = coefficients(angw[:, :q_own])
-    right_both = coefficients(angw[:, q_end:])
-    window[...] = aligned(jnp.concatenate([left_both, own_both, right_both], 1))
-    spread(0, q_lo, 8)
-    for q in (LANES, q_end - LANES, q_end):
-        spread(q)
-    spread(q_end + LANES, 0, 8)
 
     def held(h, l, q, n):
         if l == LAYERS - 1:
@@ -257,18 +244,36 @@
 
     for load in loads:
         load.wait()
+    for h in range(halves):
+        forward([h], q_own, q_end - LANES, 112, lambda h: field.at[h], 0, False)
+        if h == 0:
+            for pair in far_copies[1:]:
+                for copy in pair:
+                    copy.start()
+
+    for copy in ang_copies:
+        copy.wait()
+    left_both = coefficients(angw[:, :q_own])
+    right_both = coefficients(angw[:, q_end:])
+    window[...] = aligned(jnp.concatenate([left_both, own_both, right_both], 1))
+    spread(0, q_lo, 8)
+    for q in (LANES, q_end - LANES, q_end):
+        spread(q)
+    spread(q_end + LANES, 0, 8)
     for copy in near_copies:
         copy.wait()
+    for h in range(halves):
+        raw[h, FRONT - 8:FRONT, :] = near[h, 0]
+        raw[h, FRONT + rows:FRONT + rows + 8, :] = near[h, 1]
     edge = REACH + rows
-    both_halves = range(halves)
-    forward(both_halves, q_own - 8, q_end + 8, 104, lambda h: field.at[h], 0, False)
-
-    def emit(r):
-        for h in both_halves:
+    for h in range(halves):
+        forward([h], q_own - 8, q_own + 8, 16, lambda h: field.at[h], 0, False)
+        forward([h], q_end - 136, q_end + 8, 144, lambda h: field.at[h], 0, False)
+
+        def emit(r, h=h):
             out[pl.ds(r, 128), h * LANES:(h + 1) * LANES] = field[h, pl.ds(r + REACH - first, 128), :]
 
-    sweep(0, rows, 128, emit)
-    for h in both_halves:
+        sweep(0, rows, 128, emit)
         field[h, REACH - 16:REACH, :] = zeros(16)
         field[h, edge:edge + 24, :] = zeros(24)
         cut[0:HALF, :] = field[h, rows:rows + HALF, :]
@@ -276,9 +281,9 @@
         band(h, -HALF, 0, upper=whole)
         band(h, 0, rows, upper=whole, lower=whole)
         band(h, rows, rows + HALF, lower=cut, shift=rows)
-    backward(both_halves, q_lo, q_own + 8, 72, False)
-    backward(both_halves, q_own + 248, q_end - 248, 88, True)
-    backward(both_halves, q_end - 136, q_hi, 136, True)
+        backward([h], q_lo, q_own + 8, 144, False)
+        backward([h], q_own + 248, q_end - 248, 176, True)
+        backward([h], q_end - 136, q_hi, 136, True)
     collapse(q_own + 264, 120, False)
     for q in range(q_own + 384, q_end - 384, LANES):
         collapse(q, LANES, False)
@@ -373,6 +378,7 @@
         out_specs=(pl.BlockSpec(memory_space=pltpu.VMEM), pl.BlockSpec(memory_space=pltpu.VMEM)),
         scratch_shapes=[
             pltpu.VMEM((halves, FRONT + rows + SENT + 16, LANES), f32),
+            pltpu.VMEM((halves, 2, 8, LANES), f32),
             pltpu.VMEM((halves, 2, HALF, LANES), f32),
             pltpu.VMEM((LAYERS, total_q), f32),
             pltpu.VMEM((2 * LAYERS, total_q, LANES), f32),

time: 30.4 us -> 29.9 us (0.984)
  Pallas kernels: 27.7 us -> 27.2 us
    pallas_call x1, Pallas kernels: 27.7 us -> 27.2 us  [on_device(): pl.pallas_call(functools.partial(kernel, nblk, ncol), out_shape=(pltpu.VM...]
where the time goes in v7:
time: 29.9 us; the launch traced here: 29.8 us
  Pallas kernels  27.2 us (91%)
  local copies, waits for them, and re-layouts  1.93 us (6%)
  between operations  0.64 us (2%)
    pallas_call x1, Pallas kernels, on_device(): pl.pallas_call(functools.partial(kernel, nblk, ncol), out_shape=(pltpu.VM...  27.2 us
    unnamed x2, local copies, waits for them, and re-layouts  1.93 us

profile of v7, /device:TPU:0, one launch (start us, length us, event | category | flops | bytes accessed | tf_op | source)
XLA Modules:
  0.0 29.8 jit_solution(2058422343506425374)
XLA Ops:
  0.6 27.2 %shard_map.68 = (f32[2048,256]{1,0:T(8,128)S(1)}, f32[4,1024]{1,0:T(4,128)S(1)}) custom-call(s32[4]{0:T(128)} %pairing.1, s32[8]{0:T(128)} %offsets.1, f32[8]{0:T(128)} %weights.1, f32[2048,256]{1,0:T(8,128)} %slab.1, f32[4,1024]{1,0:T(4,128)} %angles.1), custom_call_target="tpu_custom_call" | custom-call | tf_op jit(solution)/shard_map/pallas_call | solution.py:371
  27.9 1.3 %copy.9 = f32[2048,256]{1,0:T(8,128)} copy(f32[2048,256]{1,0:T(8,128)S(1)} %get-tuple-element.2) | data formatting | bytes 4194304
  29.2 0.6 %copy.10 = f32[4,1024]{1,0:T(4,128)} copy(f32[4,1024]{1,0:T(4,128)S(1)} %get-tuple-element.3) | data formatting | bytes 32768

commit v8 on v7

--- a/solution.py
+++ b/solution.py
@@ -101,6 +101,10 @@
 
     first = pairing[0]
 
+    pl.semaphore_wait(barrier, len(peers))
+    for copy in ang_copies + near_copies + far_copies[0]:
+        copy.start()
+
     def zeros(n):
         return jnp.zeros((n, LANES), jnp.float32)
 
@@ -144,10 +148,6 @@
     window[:, q_own:q_end] = aligned(own_both)
     for q in range(q_own, q_end - LANES, LANES):
         spread(q)
-
-    pl.semaphore_wait(barrier, len(peers))
-    for copy in ang_copies + near_copies + far_copies[0]:
-        copy.start()
 
     def held(h, l, q, n):
         if l == LAYERS - 1:
@@ -246,10 +246,9 @@
         load.wait()
     for h in range(halves):
         forward([h], q_own, q_end - LANES, 112, lambda h: field.at[h], 0, False)
-        if h == 0:
-            for pair in far_copies[1:]:
-                for copy in pair:
-                    copy.start()
+    for pair in far_copies[1:]:
+        for copy in pair:
+            copy.start()
 
     for copy in ang_copies:
         copy.wait()

time: 29.9 us -> 28.9 us (0.967)
  Pallas kernels: 27.2 us -> 26.2 us
    pallas_call x1, Pallas kernels: 27.2 us -> 26.2 us  [on_device(): pl.pallas_call(functools.partial(kernel, nblk, ncol), out_shape=(pltpu.VM...]
where the time goes in v8:
time: 28.9 us; the launch traced here: 28.8 us
  Pallas kernels  26.2 us (91%)
  local copies, waits for them, and re-layouts  1.93 us (7%)
  between operations  0.64 us (2%)
    pallas_call x1, Pallas kernels, on_device(): pl.pallas_call(functools.partial(kernel, nblk, ncol), out_shape=(pltpu.VM...  26.2 us
    unnamed x2, local copies, waits for them, and re-layouts  1.93 us

profile of v8, /device:TPU:0, one launch (start us, length us, event | category | flops | bytes accessed | tf_op | source)
XLA Modules:
  0.0 28.8 jit_solution(17500970587282469244)
XLA Ops:
  0.6 26.2 %shard_map.68 = (f32[2048,256]{1,0:T(8,128)S(1)}, f32[4,1024]{1,0:T(4,128)S(1)}) custom-call(s32[4]{0:T(128)} %pairing.1, s32[8]{0:T(128)} %offsets.1, f32[8]{0:T(128)} %weights.1, f32[2048,256]{1,0:T(8,128)} %slab.1, f32[4,1024]{1,0:T(4,128)} %angles.1), custom_call_target="tpu_custom_call" | custom-call | tf_op jit(solution)/shard_map/pallas_call | solution.py:370
  26.8 1.3 %copy.9 = f32[2048,256]{1,0:T(8,128)} copy(f32[2048,256]{1,0:T(8,128)S(1)} %get-tuple-element.2) | data formatting | bytes 4194304
  28.2 0.6 %copy.10 = f32[4,1024]{1,0:T(4,128)} copy(f32[4,1024]{1,0:T(4,128)S(1)} %get-tuple-element.3) | data formatting | bytes 32768

commit v9 on v7

--- a/solution.py
+++ b/solution.py
@@ -65,7 +65,7 @@
     every = [col] + others
 
     barrier = pltpu.get_barrier_semaphore()
-    peers = [(blk, c) for c in others] + [(b, c) for b in (after, before) for c in every]
+    peers = [(b, c) for c in every for b in (after, before)] + [(blk, c) for c in others]
     for peer in peers:
         pl.semaphore_signal(barrier, inc=1, device_id=peer, device_id_type=MESH)
 
@@ -100,6 +100,10 @@
         ])
 
     first = pairing[0]
+
+    pl.semaphore_wait(barrier, len(peers))
+    for copy in ang_copies + near_copies + far_copies[0]:
+        copy.start()
 
     def zeros(n):
         return jnp.zeros((n, LANES), jnp.float32)
@@ -144,10 +148,6 @@
     window[:, q_own:q_end] = aligned(own_both)
     for q in range(q_own, q_end - LANES, LANES):
         spread(q)
-
-    pl.semaphore_wait(barrier, len(peers))
-    for copy in ang_copies + near_copies + far_copies[0]:
-        copy.start()
 
     def held(h, l, q, n):
         if l == LAYERS - 1:

time: 29.9 us -> 28.9 us (0.967)
  Pallas kernels: 27.2 us -> 26.2 us
    pallas_call x1, Pallas kernels: 27.2 us -> 26.2 us  [on_device(): pl.pallas_call(functools.partial(kernel, nblk, ncol), out_shape=(pltpu.VM...]
where the time goes in v9:
time: 28.9 us; the launch traced here: 28.7 us
  Pallas kernels  26.2 us (91%)
  local copies, waits for them, and re-layouts  1.93 us (7%)
  between operations  0.64 us (2%)
    pallas_call x1, Pallas kernels, on_device(): pl.pallas_call(functools.partial(kernel, nblk, ncol), out_shape=(pltpu.VM...  26.2 us
    unnamed x2, local copies, waits for them, and re-layouts  1.93 us

profile of v9, /device:TPU:0, one launch (start us, length us, event | category | flops | bytes accessed | tf_op | source)
XLA Modules:
  0.0 28.7 jit_solution(6903806204065646791)
XLA Ops:
  0.6 26.2 %shard_map.68 = (f32[2048,256]{1,0:T(8,128)S(1)}, f32[4,1024]{1,0:T(4,128)S(1)}) custom-call(s32[4]{0:T(128)} %pairing.1, s32[8]{0:T(128)} %offsets.1, f32[8]{0:T(128)} %weights.1, f32[2048,256]{1,0:T(8,128)} %slab.1, f32[4,1024]{1,0:T(4,128)} %angles.1), custom_call_target="tpu_custom_call" | custom-call | tf_op jit(solution)/shard_map/pallas_call | solution.py:371
  26.8 1.3 %copy.9 = f32[2048,256]{1,0:T(8,128)} copy(f32[2048,256]{1,0:T(8,128)S(1)} %get-tuple-element.2) | data formatting | bytes 4194304
  28.1 0.6 %copy.10 = f32[4,1024]{1,0:T(4,128)} copy(f32[4,1024]{1,0:T(4,128)S(1)} %get-tuple-element.3) | data formatting | bytes 32768
